TPU v7x, 512 devices: a whole 4x8x8 slice. The times are simulated.
512 devices in a mesh: scan: 32 (over z, x), tile: 16 (over y, core).
Axes of the slice: x: 4, y: 8, z: 8, core: 2. Of those that a mesh axis runs over, the one named last changes fastest.
Arguments:
- object_field: float32 [2, 512, 6144], P(None, None, 'tile'), may hold values from -6 to 6
- probe: bfloat16 [3, 2, 128, 128], replicated, may hold values from -3 to 3
- measured: float32 [4096, 128, 128], P(('scan', 'tile')), may hold values from 0 to 12
- positions: int32 [4096, 2], P(('scan', 'tile')), may hold values from 0 to 5759, as said below
Outputs:
- object_grad: float32 [2, 512, 6144], P(None, 'scan', 'tile')
- probe_grad: float32 [3, 2, 128, 128], replicated
- position_grad: float32 [4096, 2], P(('scan', 'tile'))
Inputs may be any that keep to these rules, and one draw needn't show every extreme that they name: `positions`: each column offset lies 1 to 127 columns left of the boundary between tiles k and k + 1 of 384 columns each (0 <= k <= 14), so every window covers columns of exactly two adjacent tiles; the 8 patterns of one device have different k; in every draw some k is taken by a pattern of every device of one group along tile; row offsets are at most 384.
All inputs are finite; a program needn't handle non-finite values.
Results may differ from a plain program's by a relative error of at most 0.003.
Values may be sent and summed in bfloat16 or wider, within the bound.
No kernel may reach another device: no remote copies, remote signals or barrier semaphores. Data moves between devices by JAX's collectives and lax.ppermute only.
A program may use at most 128 MiB of HBM per device.

v0:
```python
import math

import jax
import jax.numpy as jnp
from jax import lax
from jax.sharding import PartitionSpec as P


def from_behind(value, axis, steps):
    count = lax.axis_size(axis)
    first, last = (max(0, -steps), min(count, count - steps))
    return lax.ppermute(value, axis, [(source, source + steps) for source in range(first, last)])


def multiply_left(matrix, stacked):
    return jnp.einsum("ij,bjk->bik", matrix, stacked, precision=lax.Precision.HIGHEST)


def multiply_right(stacked, matrix):
    return jnp.einsum("bij,jk->bik", stacked, matrix, precision=lax.Precision.HIGHEST)


def forward_dft(real_part, imaginary_part, cosine_table, sine_table):
    left_real = multiply_left(cosine_table, real_part) + multiply_left(sine_table, imaginary_part)
    left_imaginary = multiply_left(cosine_table, imaginary_part) - multiply_left(
        sine_table, real_part
    )
    out_real = multiply_right(left_real, cosine_table) + multiply_right(left_imaginary, sine_table)
    out_imaginary = multiply_right(left_imaginary, cosine_table) - multiply_right(
        left_real, sine_table
    )
    return (out_real, out_imaginary)


def inverse_dft(real_part, imaginary_part, cosine_table, sine_table):
    left_real = multiply_left(cosine_table, real_part) - multiply_left(sine_table, imaginary_part)
    left_imaginary = multiply_left(cosine_table, imaginary_part) + multiply_left(
        sine_table, real_part
    )
    out_real = multiply_right(left_real, cosine_table) - multiply_right(left_imaginary, sine_table)
    out_imaginary = multiply_right(left_imaginary, cosine_table) + multiply_right(
        left_real, sine_table
    )
    return (out_real, out_imaginary)


def process(windows, intensity, validity, probe, cosine_table, sine_table):
    count = windows.shape[0]
    mode_count = probe.shape[0]
    window_size = probe.shape[2]
    window_full = windows.astype(jnp.float32)
    probe_real = probe[:, 0].astype(jnp.float32)[None]
    probe_imaginary = probe[:, 1].astype(jnp.float32)[None]
    window_real = window_full[:, 0][:, None]
    window_imaginary = window_full[:, 1][:, None]
    flat_shape = (count * mode_count, window_size, window_size)
    full_shape = (count, mode_count, window_size, window_size)
    exit_real = (probe_real * window_real - probe_imaginary * window_imaginary).reshape(flat_shape)
    exit_imaginary = (probe_real * window_imaginary + probe_imaginary * window_real).reshape(
        flat_shape
    )
    far_real, far_imaginary = forward_dft(exit_real, exit_imaginary, cosine_table, sine_table)
    far_real = far_real.reshape(full_shape)
    far_imaginary = far_imaginary.reshape(full_shape)
    modeled = jnp.sum(far_real**2 + far_imaginary**2, axis=1)
    scaling = (1.0 - jnp.sqrt(intensity) / jnp.maximum(jnp.sqrt(modeled), 0.5)) * validity[
        :, None, None
    ]
    back_real, back_imaginary = inverse_dft(
        (scaling[:, None] * far_real).reshape(flat_shape),
        (scaling[:, None] * far_imaginary).reshape(flat_shape),
        cosine_table,
        sine_table,
    )
    back_real = back_real.reshape(full_shape)
    back_imaginary = back_imaginary.reshape(full_shape)
    patch_grad = jnp.stack(
        [
            jnp.sum(probe_real * back_real + probe_imaginary * back_imaginary, axis=1),
            jnp.sum(probe_real * back_imaginary - probe_imaginary * back_real, axis=1),
        ],
        axis=1,
    ).astype(jnp.bfloat16)
    probe_term = jnp.stack(
        [
            jnp.sum(window_real * back_real + window_imaginary * back_imaginary, axis=0),
            jnp.sum(window_real * back_imaginary - window_imaginary * back_real, axis=0),
        ],
        axis=1,
    )
    row_change = jnp.concatenate(
        [
            window_full[:, :, 1:, :] - window_full[:, :, :-1, :],
            jnp.zeros((count, 2, 1, window_size), jnp.float32),
        ],
        axis=2,
    )
    column_change = jnp.concatenate(
        [
            window_full[:, :, :, 1:] - window_full[:, :, :, :-1],
            jnp.zeros((count, 2, window_size, 1), jnp.float32),
        ],
        axis=3,
    )

    def weighted_sum(difference):
        weighted_real = (
            probe_real * difference[:, 0][:, None] - probe_imaginary * difference[:, 1][:, None]
        )
        weighted_imaginary = (
            probe_real * difference[:, 1][:, None] + probe_imaginary * difference[:, 0][:, None]
        )
        return (
            jnp.sum(back_real * weighted_real + back_imaginary * weighted_imaginary, axis=(1, 2, 3))
            / window_size
        )

    position_grad = jnp.stack([weighted_sum(row_change), weighted_sum(column_change)], axis=1)
    return (patch_grad, probe_term, position_grad)


def deposit_all(offsets, gradients, base_column, height, extended_width):
    window_size = gradients.shape[2]

    def deposit(slot_index, accumulated):
        offset = offsets[slot_index]
        corner = (jnp.int32(0), offset[0], offset[1] - base_column)
        current = lax.dynamic_slice(accumulated, corner, (2, window_size, window_size))
        return lax.dynamic_update_slice(
            accumulated, current + gradients[slot_index].astype(jnp.float32), corner
        )

    return lax.fori_loop(
        0, gradients.shape[0], deposit, jnp.zeros((2, height, extended_width), jnp.float32)
    )


def local(object_field, probe, measured, positions):
    tile_count = lax.axis_size("tile")
    own_tile = lax.axis_index("tile")
    tile_width = object_field.shape[2]
    height = object_field.shape[1]
    window_size = probe.shape[2]
    patterns = measured.shape[0]
    total_count = patterns * lax.axis_size("scan") * tile_count
    base_column = own_tile * tile_width
    object_low = object_field.astype(jnp.bfloat16)
    margin = from_behind(object_low[:, :, :window_size], "tile", -1)
    extended = jnp.concatenate([object_low, margin], axis=2)
    ramp_values = jnp.arange(window_size, dtype=jnp.int32)
    phase_index = ramp_values[:, None] * ramp_values[None, :] % window_size
    angles = phase_index.astype(jnp.float32) * (2.0 * math.pi / window_size)
    cosine_table = jnp.cos(angles) / math.sqrt(window_size)
    sine_table = jnp.sin(angles) / math.sqrt(window_size)
    left_tile = positions[:, 1] // tile_width
    owners = jnp.arange(tile_count, dtype=jnp.int32)
    targets = owners[None, :] == left_tile[:, None]
    occupied = jnp.any(targets, axis=0)
    chosen = jnp.sum(jnp.where(targets[:, :, None], positions[:, None, :], 0), axis=0)
    spare_rows = jnp.stack([jnp.zeros_like(owners), owners * tile_width], axis=1)
    requests = jnp.where(occupied[:, None], chosen, spare_rows)

    def cut_window(offset):
        corner = (jnp.int32(0), offset[0], offset[1] - base_column)
        return lax.dynamic_slice(extended, corner, (2, window_size, window_size))

    requested = lax.all_to_all(requests, "tile", split_axis=0, concat_axis=0, tiled=True)
    pieces = jax.vmap(cut_window)(requested)
    fetched = lax.all_to_all(pieces, "tile", split_axis=0, concat_axis=0, tiled=True)
    selector = targets.astype(jnp.bfloat16)
    windows = jnp.einsum(
        "pt,tcij->pcij", selector, fetched, preferred_element_type=jnp.float32
    ).astype(jnp.bfloat16)
    patch_grad, probe_term, position_grad = process(
        windows, measured, jnp.ones((patterns,), jnp.float32), probe, cosine_table, sine_table
    )
    outgoing = jnp.einsum(
        "pt,pcij->tcij", selector, patch_grad, preferred_element_type=jnp.float32
    ).astype(jnp.bfloat16)
    returned = lax.all_to_all(outgoing, "tile", split_axis=0, concat_axis=0, tiled=True)
    accumulated = deposit_all(requested, returned, base_column, height, tile_width + window_size)
    spilled = from_behind(accumulated[:, :, tile_width:], "tile", 1)
    tile_grad = accumulated[:, :, :tile_width] + jnp.pad(
        spilled, ((0, 0), (0, 0), (0, tile_width - window_size))
    )
    probe_grad = lax.psum(probe_term, ("scan", "tile")) / math.sqrt(total_count)
    summed = lax.psum(tile_grad, "scan")
    band_rows = height // lax.axis_size("scan")
    object_grad = lax.dynamic_slice_in_dim(summed, lax.axis_index("scan") * band_rows, band_rows, 1)
    return (object_grad, probe_grad, position_grad)


def solution(mesh):
    return jax.shard_map(
        local,
        mesh=mesh,
        in_specs=(
            P(None, None, "tile"),
            P(),
            P(("scan", "tile"), None, None),
            P(("scan", "tile"), None),
        ),
        out_specs=(P(None, "scan", "tile"), P(), P(("scan", "tile"), None)),
        check_vma=False,
    )
```

profile of v0, /device:TPU:24, one launch (start us, length us, event | category | flops | bytes accessed | tf_op | source)
XLA Modules:
  0.0 766.4 jit_solution(17322610847971502941)
XLA Ops:
  9.4 8.9 %all-to-all-start = ((s32[16,1,2]{2,1,0:T(1,128)}), s32[16,1,2]{2,1,0:T(1,128)S(1)}, u32[]{:S(2)}, u32[]{:S(2)}) async-start(s32[16,1,2]{2,1,0:T(1,128)} %copy.82), calls=%async_computation | async-start | bytes 16384 | tf_op jit(solution)/shard_map/all_to_all | solution.py:167
  22.8 3.1 collective-permute-done
  26.0 41.9 %while.15 = (s32[]{:T(128)}, bf16[2,512,512]{2,1,0:T(8,128)(2,1)S(1)}, s32[16,3]{0,1:T(4,128)S(1)}, bf16[16,2,128,128]{3,2,1,0:T(8,128)(2,1)}, s32[]{:T(128)}) while((s32[]{:T(128)}, bf16[2,512,512]{2,1,0:T(8,128)(2,1)S(1)}, s32[16,3]{0,1:T(4,128)S(1)}, bf16[16,2,128,128]{3,2,1,0:T(8,128)(2,1)}, s32[]{:T(128)}) %tuple.75), condition=%wide.while_cond, body=%wide.while_body.sunk | while | flops 2 | bytes 132713 | solution.py:165
  67.9 8.6 %all-to-all-start.1 = ((bf16[16,2,128,128]{3,2,1,0:T(8,128)(2,1)}), bf16[16,2,128,128]{3,2,1,0:T(8,128)(2,1)S(1)}, u32[]{:S(2)}, u32[]{:S(2)}) async-start(bf16[16,2,128,128]{3,2,1,0:T(8,128)(2,1)} %get-tuple-element.105), calls=%async_computation.1 | async-start | bytes 2097152 | tf_op jit(solution)/shard_map/all_to_all | solution.py:169
  76.6 26.2 %all-to-all-done.1 = bf16[16,2,128,128]{3,2,1,0:T(8,128)(2,1)S(1)} async-done(((bf16[16,2,128,128]{3,2,1,0:T(8,128)(2,1)}), bf16[16,2,128,128]{3,2,1,0:T(8,128)(2,1)S(1)}, u32[]{:S(2)}, u32[]{:S(2)}) %all-to-all-start.1) | async-done | bytes 1048608 | tf_op jit(solution)/shard_map/all_to_all | solution.py:169
  113.0 3.2 fusion.14
  124.6 4.5 multiply_add_fusion.2
  144.0 3.0 fusion.4
  157.5 4.3 multiply_subtract_fusion
  163.9 5.2 all-to-all-start.2
  169.2 26.3 %all-to-all-done.2 = bf16[16,2,128,128]{3,2,1,0:T(8,128)(2,1)} async-done(((bf16[16,2,128,128]{3,2,1,0:T(8,128)(2,1)}), bf16[16,2,128,128]{3,2,1,0:T(8,128)(2,1)}, u32[]{:S(2)}, u32[]{:S(2)}) %all-to-all-start.2) | async-done | bytes 1048608 | tf_op jit(solution)/shard_map/all_to_all | solution.py:180
  197.1 122.1 %while.14 = (s32[]{:T(128)}, f32[2,512,512]{2,1,0:T(8,128)}, s32[16,2]{0,1:T(2,128)S(1)}, s32[]{:T(128)}, bf16[16,2,128,128]{3,2,1,0:T(8,128)(2,1)}, /*index=5*/s32[]{:T(128)}, s32[]{:T(128)}, s32[]{:T(128)}) while((s32[]{:T(128)}, f32[2,512,512]{2,1,0:T(8,128)}, s32[16,2]{0,1:T(2,128)S(1)}, s32[]{:T(128)}, ...), condition=%wide.region_6.7_spmd, body=%wide.region_5.6_spmd.sunk | while | flops 65545 | bytes 590041 | solution.py:133
  201.3 3.3 dynamic_update_slice.8
  208.8 3.7 dynamic_update_slice.8
  216.7 3.7 dynamic_update_slice.8
  224.6 3.3 dynamic_update_slice.8
  232.1 3.3 dynamic_update_slice.8
  239.6 3.7 dynamic_update_slice.8
  247.4 3.3 dynamic_update_slice.8
  254.9 3.7 dynamic_update_slice.8
  262.8 3.3 dynamic_update_slice.8
  270.3 3.3 dynamic_update_slice.8
  277.8 3.3 dynamic_update_slice.8
  285.3 3.3 dynamic_update_slice.8
  292.7 3.3 dynamic_update_slice.8
  300.2 3.7 dynamic_update_slice.8
  308.1 3.3 dynamic_update_slice.8
  315.6 3.7 dynamic_update_slice.8
  325.2 6.8 collective-permute-done.1
  334.9 3.4 fusion.3
  339.3 255.9 %all-reduce.9.cloned.1.call-done = f32[3,2,128,128]{3,2,1,0:T(8,128)} async-done(((f32[3,2,128,128]{3,2,1,0:T(8,128)}), f32[3,2,128,128]{3,2,1,0:T(8,128)}) %all-reduce.9.cloned.1.call-update) | async-done | bytes 393232 | tf_op jit(solution)/shard_map/psum | solution.py:186
  597.0 160.7 %all-reduce.7.cloned.1.call-done = f32[2,512,384]{2,1,0:T(8,128)} async-done(((f32[2,512,384]{2,1,0:T(8,128)}), f32[2,512,384]{2,1,0:T(8,128)}) %all-reduce.7.cloned.1.call-update) | async-done | bytes 1572880 | tf_op jit(solution)/shard_map/psum | solution.py:187
  (176 shorter events, 136.3 us)
Async XLA Ops:
  9.4 13.3 %all-to-all-start = ((s32[16,1,2]{2,1,0:T(1,128)}), s32[16,1,2]{2,1,0:T(1,128)S(1)}, u32[]{:S(2)}, u32[]{:S(2)}) async-start(s32[16,1,2]{2,1,0:T(1,128)} %copy.82), calls=%async_computation | async-start | bytes 16384 | tf_op jit(solution)/shard_map/all_to_all | solution.py:167
  19.8 6.1 collective-permute-start
  26.0 50.5 %copy-start.6 = (bf16[3,2,128,128]{3,2,1,0:T(8,128)(2,1)S(1)}, bf16[3,2,128,128]{3,2,1,0:T(8,128)(2,1)}, u32[]{:S(2)}) copy-start(bf16[3,2,128,128]{3,2,1,0:T(8,128)(2,1)} %param.7) | copy-start | bytes 589828
  67.9 34.8 %all-to-all-start.1 = ((bf16[16,2,128,128]{3,2,1,0:T(8,128)(2,1)}), bf16[16,2,128,128]{3,2,1,0:T(8,128)(2,1)S(1)}, u32[]{:S(2)}, u32[]{:S(2)}) async-start(bf16[16,2,128,128]{3,2,1,0:T(8,128)(2,1)} %get-tuple-element.105), calls=%async_computation.1 | async-start | bytes 2097152 | tf_op jit(solution)/shard_map/all_to_all | solution.py:169
  103.6 0.8 copy-start.1
  103.7 0.8 copy-start.3
  130.8 1.6 copy-start
  156.3 1.0 copy-start.2
  156.3 1.2 copy-start.4
  163.9 31.6 %all-to-all-start.2 = ((bf16[16,2,128,128]{3,2,1,0:T(8,128)(2,1)}), bf16[16,2,128,128]{3,2,1,0:T(8,128)(2,1)}, u32[]{:S(2)}, u32[]{:S(2)}) async-start(bf16[16,2,128,128]{3,2,1,0:T(8,128)(2,1)} %copy.105), calls=%async_computation.2 | async-start | bytes 2097152 | tf_op jit(solution)/shard_map/all_to_all | solution.py:180
  169.2 426.1 %all-reduce.9.cloned.1.call-start = ((), (), s32[]{:S(2)}) async-start(), calls=%async_computation.4 | async-start | bytes 786432 | tf_op jit(solution)/shard_map/psum | solution.py:186
  197.1 126.3 %copy-start.5 = (f32[3,128,128]{2,1,0:T(8,128)S(1)}, f32[3,128,128]{2,1,0:T(8,128)}, u32[]{:S(2)}) copy-start(f32[3,128,128]{2,1,0:T(8,128)} %get-tuple-element.162) | copy-start | bytes 589828
  321.2 10.8 %collective-permute-start.1 = (f32[2,512,128]{2,1,0:T(8,128)}, f32[2,512,128]{2,1,0:T(8,128)}, u32[]{:S(2)}, u32[]{:S(2)}) collective-permute-start(f32[2,512,128]{2,1,0:T(8,128)} %slice.83), channel_id=1, source_target_pairs={{0,1},{1,2},{2,3},{3,4},{4,5},{5,6},{6,7},{7,8},{8,9},{9,10},{10,1... | collective-permute-start | bytes 1572872 | tf_op jit(solution)/shard_map/ppermute | solution.py:12
  325.1 432.6 %all-reduce.7.cloned.1.call-start = ((), (), s32[]{:S(2)}) async-start(), calls=%async_computation.3 | async-start | bytes 3145728 | tf_op jit(solution)/shard_map/psum | solution.py:187
Sparse Core Ops, SparseCore 0:
  325.3 269.9 all-reduce.8
  599.0 158.6 all-reduce.6
where the time goes:
time: 779 us; the launch traced here: 766 us
  waiting for transfers between devices  480 us (62%)
  local copies, waits for them, and re-layouts  116 us (15%)
  matrix products  48.3 us (6%)
  loops' own time  40.4 us (5%)
  other arithmetic  39.8 us (5%)
  starting transfers between devices  27.2 us (3%)
  between operations  14.9 us (2%)
    psum x1, waiting for transfers between devices, local(): probe_grad = lax.psum(probe_term, ('scan', 'tile')) / math.sqrt(total_count)  256 us
    psum x1, waiting for transfers between devices, local(): summed = lax.psum(tile_grad, 'scan')  161 us
    dynamic_update_slice x16, local copies, waits for them, and re-layouts, deposit(): lax.dynamic_update_slice(accumulated, current + gradients[slot_index].ast...  54.8 us
    gather x48, local copies, waits for them, and re-layouts  41.8 us
    another operation x1, loops' own time, deposit_all(): lax.fori_loop(0, gradients.shape[0], deposit, jnp.zeros((2, height, exten...  40.3 us
    all_to_all x1, waiting for transfers between devices, local(): lax.all_to_all(outgoing, 'tile', split_axis=0, concat_axis=0, tiled=True)  26.3 us
    all_to_all x1, waiting for transfers between devices, local(): lax.all_to_all(pieces, 'tile', split_axis=0, concat_axis=0, tiled=True)  26.2 us
    dot_general x8, matrix products, multiply_right(): jnp.einsum('bij,jk->bik', stacked, matrix, precision=lax.Precision.HIGHEST)  24.7 us
  transfers between devices with their start and end apart: 7, of which 7 were waited for; matrix products, arithmetic and copies ran while one was open for 2% of the time, Pallas kernels for 0%

commit v1 on v0

v1 whole, which is shorter than its diff:
```python
import math

import jax
import jax.numpy as jnp
import numpy as np
from jax import lax
from jax.experimental import pallas as pl
from jax.experimental.pallas import tpu as pltpu
from jax.sharding import PartitionSpec as P

F32 = jnp.float32
BF16 = jnp.bfloat16
TOP = math.sqrt(12.0)
STEPS = 65535.0
HALF = 32768.0


def dft_tables(window):
    ramp = np.arange(window)
    angles = (ramp[:, None] * ramp[None, :] % window) * (2.0 * np.pi / window)
    cosine = np.cos(angles) / np.sqrt(window)
    sine = np.sin(angles) / np.sqrt(window)
    first = np.block([[cosine, -sine], [sine, cosine]])
    second = np.block([[cosine, sine], [-sine, cosine]])
    tables = []
    for table in (first, second):
        high = table.astype(np.float32).astype(BF16)
        low = (table - high.astype(np.float64)).astype(np.float32).astype(BF16)
        tables.append(np.concatenate([high, high, low], axis=0))
        tables.append(np.concatenate([high, high, low], axis=1))
    return tables


def split(value):
    high = value.astype(BF16)
    return high, (value - high.astype(F32)).astype(BF16)


def from_right(value, table):
    high, low = split(value)
    return jnp.dot(
        jnp.concatenate([high, low, high], axis=1), table, preferred_element_type=F32
    )


def from_left(table, value):
    high, low = split(value)
    return jnp.dot(
        table, jnp.concatenate([high, low, high], axis=0), preferred_element_type=F32
    )


def pack_kernel(positions, measured, packed):
    patterns = measured.shape[0]
    slots, rows, window = packed.shape
    packed[...] = jnp.zeros(packed.shape, jnp.int16)
    lane = lax.broadcasted_iota(jnp.int32, (rows - window, window), 1)
    for p in range(patterns):
        row = positions[p, 0]
        column = positions[p, 1]
        tile = column // (3 * window)
        start = column - tile * (3 * window) - 2 * window
        amplitude = jnp.sqrt(measured[p]) * (STEPS / TOP)
        level = jnp.clip(jnp.round(amplitude) - HALF, -HALF, HALF - 1.0)
        packed[tile, 0:window, :] = level.astype(jnp.int32).astype(jnp.int16)
        note = jnp.where(lane == 0, row, jnp.where(lane == 1, start, jnp.where(lane == 2, 1, 0)))
        packed[tile, window:rows, :] = note.astype(jnp.int16)


def main_kernel(
    notes, received, own, margin, probe, first_down, first_across, second_down, second_across,
    sums, shifts, strip, total, probe_total, probe_full,
):
    slots = received.shape[0]
    modes = probe.shape[0]
    window = probe.shape[2]
    bands = sums.shape[0]
    height = own.shape[1]
    for part in range(2):
        strip[part, 0] = own[part].astype(BF16).astype(F32)
        strip[part, 1] = margin[part].astype(F32)
        for m in range(modes):
            probe_full[m, part] = probe[m, part].astype(F32)
    total[...] = jnp.zeros(total.shape, F32)
    probe_total[...] = jnp.zeros(probe_total.shape, F32)
    lane = lax.broadcasted_iota(jnp.int32, (window, window), 1)
    row = lax.broadcasted_iota(jnp.int32, (window, window), 0)

    def one(slot):
        start_row = notes[slot, 0]
        start = jnp.clip(notes[slot, 1], 1, window - 1)
        valid = notes[slot, 2].astype(F32)
        rows = pl.ds(start_row, window)
        cut = []
        for part in range(2):
            near = pltpu.roll(strip[part, 0, rows, :], window - start, 1)
            far = pltpu.roll(strip[part, 1, rows, :], window - start, 1)
            cut.append(jnp.where(lane < window - start, near, far))
        w_re, w_im = cut
        exits = []
        for m in range(modes):
            p_re, p_im = probe_full[m, 0], probe_full[m, 1]
            exits.append(
                jnp.concatenate([p_re * w_re - p_im * w_im, p_re * w_im + p_im * w_re], axis=1)
            )
        half = from_right(jnp.concatenate(exits, axis=0), first_down[...])
        stacked = jnp.concatenate(
            [
                jnp.concatenate(
                    [half[m * window:(m + 1) * window, c * window:(c + 1) * window] for m in range(modes)],
                    axis=1,
                )
                for c in range(2)
            ],
            axis=0,
        )
        field = from_left(second_across[...], stacked)
        power = jnp.zeros((window, window), F32)
        for m in range(modes):
            for c in range(2):
                piece = field[c * window:(c + 1) * window, m * window:(m + 1) * window]
                power = power + piece * piece
        amplitude = (received[slot, 0:window, :].astype(jnp.int32).astype(F32) + HALF) * (TOP / STEPS)
        scaling = valid * (1.0 - amplitude * lax.rsqrt(jnp.maximum(power, 0.25)))
        scaled = jnp.concatenate(
            [
                jnp.concatenate(
                    [
                        scaling * field[c * window:(c + 1) * window, m * window:(m + 1) * window]
                        for c in range(2)
                    ],
                    axis=1,
                )
                for m in range(modes)
            ],
            axis=0,
        )
        half = from_right(scaled, second_down[...])
        stacked = jnp.concatenate(
            [
                jnp.concatenate(
                    [half[m * window:(m + 1) * window, c * window:(c + 1) * window] for m in range(modes)],
                    axis=1,
                )
                for c in range(2)
            ],
            axis=0,
        )
        back = from_left(first_across[...], stacked)
        patch_re = jnp.zeros((window, window), F32)
        patch_im = jnp.zeros((window, window), F32)
        for m in range(modes):
            p_re, p_im = probe_full[m, 0], probe_full[m, 1]
            b_re = back[0:window, m * window:(m + 1) * window]
            b_im = back[window:, m * window:(m + 1) * window]
            patch_re = patch_re + (p_re * b_re + p_im * b_im)
            patch_im = patch_im + (p_re * b_im - p_im * b_re)
            probe_total[2 * m] += w_re * b_re + w_im * b_im
            probe_total[2 * m + 1] += w_re * b_im - w_im * b_re
        for axis, at in ((0, row), (1, lane)):
            change = patch_re * (pltpu.roll(w_re, window - 1, axis) - w_re) + patch_im * (
                pltpu.roll(w_im, window - 1, axis) - w_im
            )
            change = jnp.where(at < window - 1, change, 0.0)
            shifts[slot, pl.ds(axis, 1), :] = jnp.sum(change, axis=0, keepdims=True)
        for part, patch in enumerate((patch_re, patch_im)):
            turned = pltpu.roll(patch.astype(BF16).astype(F32), start, 1)
            total[part, 0, rows, :] += jnp.where(lane >= start, turned, 0.0)
            total[part, 1, rows, :] += jnp.where(lane < start, turned, 0.0)

    def step(at, carry):
        one(at)
        return carry

    shifts[...] = jnp.zeros(shifts.shape, F32)
    lax.fori_loop(0, slots, step, 0)
    deep = height // bands
    piece = 2 * modes * window // bands
    for b in range(bands):
        for part in range(2):
            for side in range(2):
                at = (2 * part + side) * deep
                sums[b, at:at + deep, :] = total[part, side, b * deep:(b + 1) * deep, :].astype(BF16)
        mode, offset = divmod(b * piece, window)
        parts = []
        left = piece
        while left:
            take = min(left, window - offset)
            parts.append(probe_total[mode, offset:offset + take, :])
            mode, offset, left = mode + 1, 0, left - take
        parts.append(jnp.zeros((sums.shape[1] - 4 * deep - piece, window), F32))
        sums[b, 4 * deep:, :] = jnp.concatenate(parts, axis=0).astype(BF16)


def pack(positions, measured, slots):
    window = measured.shape[2]
    return pl.pallas_call(
        pack_kernel,
        out_shape=jax.ShapeDtypeStruct((slots, window + 16, window), jnp.int16),
        in_specs=[
            pl.BlockSpec(memory_space=pltpu.SMEM),
            pl.BlockSpec(memory_space=pltpu.VMEM),
        ],
        out_specs=pl.BlockSpec(memory_space=pltpu.VMEM),
        compiler_params=pltpu.CompilerParams(vmem_limit_bytes=16 * 2**20),
    )(positions, measured)


def compute(notes, received, object_field, margin, probe, bands):
    modes, window = probe.shape[0], probe.shape[2]
    slots = received.shape[0]
    height = object_field.shape[1]
    tables = [jnp.asarray(table) for table in dft_tables(window)]
    vmem = pl.BlockSpec(memory_space=pltpu.VMEM)

    def whole(shape):
        return pl.BlockSpec(shape, lambda i: (0,) * len(shape))

    rows = 4 * (height // bands) + -(-(2 * modes * window // bands) // 16) * 16
    return pl.pallas_call(
        main_kernel,
        grid=(1,),
        out_shape=(
            jax.ShapeDtypeStruct((bands, rows, window), BF16),
            jax.ShapeDtypeStruct((slots, 8, window), F32),
        ),
        in_specs=[
            pl.BlockSpec(memory_space=pltpu.SMEM),
            whole(received.shape),
            pl.BlockSpec((2, height, window), lambda i: (0, 0, 2)),
            whole(margin.shape),
            whole(probe.shape),
        ] + [whole(table.shape) for table in tables],
        out_specs=(whole((bands, rows, window)), whole((slots, 8, window))),
        scratch_shapes=[
            pltpu.VMEM((2, 2, height, window), F32),
            pltpu.VMEM((2, 2, height, window), F32),
            pltpu.VMEM((2 * modes, window, window), F32),
            pltpu.VMEM((modes, 2, window, window), F32),
        ],
        compiler_params=pltpu.CompilerParams(vmem_limit_bytes=40 * 2**20),
    )(notes, received, object_field, margin, probe, *tables)


def exchange(value, axis):
    return lax.all_to_all(value, axis, split_axis=0, concat_axis=0, tiled=True)


def local(object_field, probe, measured, positions):
    tiles = lax.axis_size("tile")
    bands = lax.axis_size("scan")
    width = object_field.shape[2]
    height = object_field.shape[1]
    modes, window = probe.shape[0], probe.shape[2]
    patterns = measured.shape[0]
    deep = height // bands
    piece = 2 * modes * window // bands
    margin = lax.ppermute(
        object_field[:, :, :window].astype(BF16), "tile", [(t, t - 1) for t in range(1, tiles)]
    )
    received = exchange(pack(positions, measured, tiles), "tile")
    notes = received[:, window, :3].astype(jnp.int32)
    sums, shifts = compute(notes, received, object_field, margin, probe, bands)
    gathered = jnp.sum(exchange(sums, "scan").astype(F32), axis=0)
    strips = gathered[:4 * deep].reshape(2, 2, deep, window)
    spilled = lax.ppermute(strips[:, 1], "tile", [(t, t + 1) for t in range(tiles - 1)])
    object_grad = jnp.concatenate(
        [spilled, jnp.zeros((2, deep, width - 2 * window), F32), strips[:, 0]], axis=2
    )
    own_piece = gathered[4 * deep:4 * deep + piece]
    outgoing = jnp.concatenate(
        [jnp.broadcast_to(own_piece[None], (tiles, piece, window)), shifts], axis=1
    )
    mixed = exchange(outgoing, "tile")
    full_piece = jnp.sum(mixed[:, :piece], axis=0) / math.sqrt(patterns * bands * tiles)
    probe_grad = exchange(
        jnp.broadcast_to(full_piece[None], (bands, piece, window)), "scan"
    ).reshape(modes, 2, window, window)
    per_tile = jnp.sum(mixed[:, piece:piece + 2], axis=2) / window
    left_tile = positions[:, 1] // width
    hits = left_tile[:, None] == jnp.arange(tiles, dtype=jnp.int32)[None, :]
    position_grad = jnp.sum(jnp.where(hits[:, :, None], per_tile[None], 0.0), axis=1)
    return (object_grad, probe_grad, position_grad)


def solution(mesh):
    return jax.shard_map(
        local,
        mesh=mesh,
        in_specs=(
            P(None, None, "tile"),
            P(),
            P(("scan", "tile"), None, None),
            P(("scan", "tile"), None),
        ),
        out_specs=(P(None, "scan", "tile"), P(), P(("scan", "tile"), None)),
        check_vma=False,
    )
```

time: 779 us -> 143 us (0.18)
  the two profiles are of different devices: /device:TPU:24 before, /device:TPU:1 now
where the time goes in v1:
time: 143 us; the launch traced here: 142 us
  waiting for transfers between devices  37.7 us (26%)
  Pallas kernels  34.2 us (24%)
  blocking collectives  33 us (23%)
  starting transfers between devices  27.8 us (19%)
  local copies, waits for them, and re-layouts  6.23 us (4%)
  other arithmetic  2.35 us (2%)
    all_to_all x3, waiting for transfers between devices, exchange(): return lax.all_to_all(value, axis, split_axis=0, concat_axis=0, tiled=True)  37.7 us
    all_to_all x1, blocking collectives, exchange(): return lax.all_to_all(value, axis, split_axis=0, concat_axis=0, tiled=True)  33 us
    pallas_call x1, Pallas kernels, compute(): pl.pallas_call(main_kernel, grid=(1,), out_shape=(jax.ShapeDtypeStruct((b...  32.5 us
    all_to_all x3, starting transfers between devices, exchange(): return lax.all_to_all(value, axis, split_axis=0, concat_axis=0, tiled=True)  22.1 us
    unnamed x19, local copies, waits for them, and re-layouts  4.68 us
    ppermute x1, starting transfers between devices, local(): lax.ppermute(strips[:, 1], 'tile', [(t, t + 1) for t in range(tiles - 1)])  3.54 us
  transfers between devices with their start and end apart: 5, of which 3 were waited for; matrix products, arithmetic and copies ran while one was open for 2% of the time, Pallas kernels for 0%

profile of v1, /device:TPU:1, one launch (start us, length us, event | category | flops | bytes accessed | tf_op | source)
XLA Modules:
  0.0 142.1 jit_solution(14373855162839886267)
XLA Ops:
  0.6 0.0 copy-start
  0.6 0.9 copy.29.positions
  1.5 1.0 copy-done.1
  2.6 1.7 %shard_map.103 = s16[16,144,128]{2,1,0:T(8,128)(2,1)} custom-call(s32[8,2]{1,0:T(8,128)S(1)} %copy.29.positions, f32[8,128,128]{2,1,0:T(8,128)S(1)} %copy-done.1), custom_call_target="tpu_custom_call" | custom-call | tf_op jit(solution)/shard_map/pallas_call | solution.py:197
  4.3 10.2 %all-to-all-start = ((s16[16,144,128]{2,1,0:T(8,128)(2,1)}), s16[16,144,128]{2,1,0:T(8,128)(2,1)S(1)}, u32[]{:S(2)}, u32[]{:S(2)}) async-start(s16[16,144,128]{2,1,0:T(8,128)(2,1)} %shard_map.103), calls=%async_computation | async-start | bytes 1179648 | tf_op jit(solution)/shard_map/all_to_all | solution.py:246
  14.6 0.0 copy-done
  14.6 0.7 slice.52
  15.3 2.1 %collective-permute-start = (bf16[2,512,128]{2,1,0:T(8,128)(2,1)}, bf16[2,512,128]{2,1,0:T(8,128)(2,1)}, u32[]{:S(2)}, u32[]{:S(2)}) collective-permute-start(bf16[2,512,128]{2,1,0:T(8,128)(2,1)} %slice.52), channel_id=1, source_target_pairs={{1,0},{2,1},{3,2},{4,3},{5,4},{6,5},{7,6},{8,7},{9,8},{10,9},{11,1... | collective-permute-start | bytes 786440 | tf_op jit(solution)/shard_map/ppermute | solution.py:258
  17.4 15.8 %all-to-all-done.received = s16[16,144,128]{2,1,0:T(8,128)(2,1)S(1)} async-done(((s16[16,144,128]{2,1,0:T(8,128)(2,1)}), s16[16,144,128]{2,1,0:T(8,128)(2,1)S(1)}, u32[]{:S(2)}, u32[]{:S(2)}) %all-to-all-start) | async-done | bytes 589856 | tf_op jit(solution)/shard_map/all_to_all | solution.py:246
  33.2 0.0 collective-permute-done.margin
  33.2 0.0 copy-done.2
  33.2 0.0 copy-start.5
  33.3 1.0 copy-done.5
  34.3 0.9 copy-done.6
  35.2 32.5 %shard_map.104 = (bf16[32,96,128]{2,1,0:T(8,128)(2,1)S(1)}, f32[16,8,128]{2,1,0:T(8,128)S(1)}) custom-call(s32[16,3]{1,0:T(8,128)S(1)} %bitcast.11, s16[16,144,128]{2,1,0:T(8,128)(2,1)S(1)} %all-to-all-done.received, f32[2,512,384]{2,1,0:T(8,128)S(1)} %copy-done, bf16[2,512,128]{2,1,0:T(8,128)(2,1)} %collective-permute-done.margin, ...), custom_call_target="tpu_custom_call" | custom-call | tf_op jit(solution)/shard_map/pallas_call | solution.py:220
  67.6 0.0 copy-start.7
  67.7 33.0 %all_to_all.20 = bf16[32,96,128]{2,1,0:T(8,128)(2,1)S(1)} all-to-all(bf16[32,96,128]{2,1,0:T(8,128)(2,1)S(1)} %get-tuple-element.5), channel_id=1, replica_groups=mesh['scan'=32,'tile'=16] {'scan'}, dimensions={0} | all-to-all | bytes 1572864 | tf_op jit(solution)/shard_map/all_to_all | solution.py:246
  100.7 0.1 convert_reduce_fusion
  100.8 0.7 pad_maximum_fusion
  101.6 6.7 %all-to-all-start.2 = ((f32[16,32,128]{2,1,0:T(8,128)}), f32[16,32,128]{2,1,0:T(8,128)S(1)}, u32[]{:S(2)}, u32[]{:S(2)}) async-start(f32[16,32,128]{2,1,0:T(8,128)} %pad_maximum_fusion), calls=%async_computation.2 | async-start | bytes 524288 | tf_op jit(solution)/shard_map/all_to_all | solution.py:246
  108.3 3.5 %collective-permute-start.1 = (f32[2,16,128]{2,1,0:T(8,128)S(1)}, f32[2,16,128]{2,1,0:T(8,128)S(1)}, u32[]{:S(2)}, u32[]{:S(2)}) collective-permute-start(f32[2,16,128]{2,1,0:T(8,128)S(1)} %get-tuple-element.7), channel_id=1, source_target_pairs={{0,1},{1,2},{2,3},{3,4},{4,5},{5,6},{6,7},{7,8},{8,9},{9,10},{10,1... | collective-permute-start | bytes 49160 | tf_op jit(solution)/shard_map/ppermute | solution.py:266
  111.8 8.4 %all-to-all-done.2 = f32[16,32,128]{2,1,0:T(8,128)S(1)} async-done(((f32[16,32,128]{2,1,0:T(8,128)}), f32[16,32,128]{2,1,0:T(8,128)S(1)}, u32[]{:S(2)}, u32[]{:S(2)}) %all-to-all-start.2) | async-done | bytes 262176 | tf_op jit(solution)/shard_map/all_to_all | solution.py:246
  120.2 0.8 broadcast_in_dim.41
  121.0 5.2 %all-to-all-start.3 = ((f32[32,24,128]{2,1,0:T(8,128)}), f32[32,24,128]{2,1,0:T(8,128)S(1)}, u32[]{:S(2)}, u32[]{:S(2)}) async-start(f32[32,24,128]{2,1,0:T(8,128)} %broadcast_in_dim.41), calls=%async_computation.3 | async-start | bytes 786432 | tf_op jit(solution)/shard_map/all_to_all | solution.py:246
  126.2 0.1 iota_compare_fusion
  126.3 0.0 collective-permute-done.1
  126.3 0.6 pad_maximum_fusion.1
  126.9 0.1 slice_reduce_fusion.1
  127.0 0.1 copy.35
  127.1 0.7 select_reduce_fusion
  127.8 13.6 %all-to-all-done.3 = f32[32,24,128]{2,1,0:T(8,128)S(1)} async-done(((f32[32,24,128]{2,1,0:T(8,128)}), f32[32,24,128]{2,1,0:T(8,128)S(1)}, u32[]{:S(2)}, u32[]{:S(2)}) %all-to-all-start.3) | async-done | bytes 393248 | tf_op jit(solution)/shard_map/all_to_all | solution.py:246
  141.4 0.7 copy.38
  (19 shorter events, 0.1 us)
Async XLA Ops:
  0.6 13.9 %copy-start = (f32[2,512,384]{2,1,0:T(8,128)S(1)}, f32[2,512,384]{2,1,0:T(8,128)}, u32[]{:S(2)}) copy-start(f32[2,512,384]{2,1,0:T(8,128)} %own.1) | copy-start | bytes 4718596
  1.5 1.0 copy-start.1
  2.6 30.7 %copy-start.2 = (bf16[768,256]{1,0:T(8,128)(2,1)S(1)}, bf16[768,256]{1,0:T(8,128)(2,1)}, u32[]{:S(2)}) copy-start(bf16[768,256]{1,0:T(8,128)(2,1)} %constant.28.clone.first_down) | copy-start | bytes 1179652
  2.6 30.7 %copy-start.3 = (bf16[256,768]{1,0:T(8,128)(2,1)S(1)}, bf16[256,768]{1,0:T(8,128)(2,1)}, u32[]{:S(2)}) copy-start(bf16[256,768]{1,0:T(8,128)(2,1)} %constant.29.clone.first_across) | copy-start | bytes 1179652
  2.6 30.7 %copy-start.4 = (bf16[768,256]{1,0:T(8,128)(2,1)S(1)}, bf16[768,256]{1,0:T(8,128)(2,1)}, u32[]{:S(2)}) copy-start(bf16[768,256]{1,0:T(8,128)(2,1)} %constant.30.clone.second_down) | copy-start | bytes 1179652
  4.3 28.9 %all-to-all-start = ((s16[16,144,128]{2,1,0:T(8,128)(2,1)}), s16[16,144,128]{2,1,0:T(8,128)(2,1)S(1)}, u32[]{:S(2)}, u32[]{:S(2)}) async-start(s16[16,144,128]{2,1,0:T(8,128)(2,1)} %shard_map.103), calls=%async_computation | async-start | bytes 1179648 | tf_op jit(solution)/shard_map/all_to_all | solution.py:246
  15.3 17.9 %collective-permute-start = (bf16[2,512,128]{2,1,0:T(8,128)(2,1)}, bf16[2,512,128]{2,1,0:T(8,128)(2,1)}, u32[]{:S(2)}, u32[]{:S(2)}) collective-permute-start(bf16[2,512,128]{2,1,0:T(8,128)(2,1)} %slice.52), channel_id=1, source_target_pairs={{1,0},{2,1},{3,2},{4,3},{5,4},{6,5},{7,6},{8,7},{9,8},{10,9},{11,1... | collective-permute-start | bytes 786440 | tf_op jit(solution)/shard_map/ppermute | solution.py:258
  33.2 1.0 copy-start.5
  34.2 0.9 copy-start.6
  67.6 40.6 %copy-start.7 = (s32[8,2]{0,1:T(2,128)S(1)}, s32[8,2]{0,1:T(2,128)}, u32[]{:S(2)}) copy-start(s32[8,2]{0,1:T(2,128)} %param.11) | copy-start | bytes 196
  101.6 18.6 %all-to-all-start.2 = ((f32[16,32,128]{2,1,0:T(8,128)}), f32[16,32,128]{2,1,0:T(8,128)S(1)}, u32[]{:S(2)}, u32[]{:S(2)}) async-start(f32[16,32,128]{2,1,0:T(8,128)} %pad_maximum_fusion), calls=%async_computation.2 | async-start | bytes 524288 | tf_op jit(solution)/shard_map/all_to_all | solution.py:246
  108.3 18.0 %collective-permute-start.1 = (f32[2,16,128]{2,1,0:T(8,128)S(1)}, f32[2,16,128]{2,1,0:T(8,128)S(1)}, u32[]{:S(2)}, u32[]{:S(2)}) collective-permute-start(f32[2,16,128]{2,1,0:T(8,128)S(1)} %get-tuple-element.7), channel_id=1, source_target_pairs={{0,1},{1,2},{2,3},{3,4},{4,5},{5,6},{6,7},{7,8},{8,9},{9,10},{10,1... | collective-permute-start | bytes 49160 | tf_op jit(solution)/shard_map/ppermute | solution.py:266
  121.0 20.4 %all-to-all-start.3 = ((f32[32,24,128]{2,1,0:T(8,128)}), f32[32,24,128]{2,1,0:T(8,128)S(1)}, u32[]{:S(2)}, u32[]{:S(2)}) async-start(f32[32,24,128]{2,1,0:T(8,128)} %broadcast_in_dim.41), calls=%async_computation.3 | async-start | bytes 786432 | tf_op jit(solution)/shard_map/all_to_all | solution.py:246

commit v2 on v1

--- a/solution.py
+++ b/solution.py
@@ -13,6 +13,7 @@
 TOP = math.sqrt(12.0)
 STEPS = 65535.0
 HALF = 32768.0
+GROUP = 16
 
 
 def dft_tables(window):
@@ -26,8 +27,8 @@
     for table in (first, second):
         high = table.astype(np.float32).astype(BF16)
         low = (table - high.astype(np.float64)).astype(np.float32).astype(BF16)
-        tables.append(np.concatenate([high, high, low], axis=0))
-        tables.append(np.concatenate([high, high, low], axis=1))
+        tables.append(np.concatenate([high, low], axis=0))
+        tables.append(np.concatenate([high, low], axis=1))
     return tables
 
 
@@ -37,17 +38,13 @@
 
 
 def from_right(value, table):
-    high, low = split(value)
-    return jnp.dot(
-        jnp.concatenate([high, low, high], axis=1), table, preferred_element_type=F32
-    )
+    high = value.astype(BF16)
+    return jnp.dot(jnp.concatenate([high, high], axis=1), table, preferred_element_type=F32)
 
 
 def from_left(table, value):
-    high, low = split(value)
-    return jnp.dot(
-        table, jnp.concatenate([high, low, high], axis=0), preferred_element_type=F32
-    )
+    high = value.astype(BF16)
+    return jnp.dot(table, jnp.concatenate([high, high], axis=0), preferred_element_type=F32)
 
 
 def pack_kernel(positions, measured, packed):
@@ -86,73 +83,42 @@
     lane = lax.broadcasted_iota(jnp.int32, (window, window), 1)
     row = lax.broadcasted_iota(jnp.int32, (window, window), 0)
 
-    def one(slot):
-        start_row = notes[slot, 0]
+    def cut(slot):
         start = jnp.clip(notes[slot, 1], 1, window - 1)
-        valid = notes[slot, 2].astype(F32)
-        rows = pl.ds(start_row, window)
-        cut = []
+        rows = pl.ds(notes[slot, 0], window)
+        both = []
         for part in range(2):
             near = pltpu.roll(strip[part, 0, rows, :], window - start, 1)
             far = pltpu.roll(strip[part, 1, rows, :], window - start, 1)
-            cut.append(jnp.where(lane < window - start, near, far))
-        w_re, w_im = cut
+            both.append(jnp.where(lane < window - start, near, far))
+        return both
+
+    def leave(w_re, w_im):
         exits = []
         for m in range(modes):
             p_re, p_im = probe_full[m, 0], probe_full[m, 1]
             exits.append(
                 jnp.concatenate([p_re * w_re - p_im * w_im, p_re * w_im + p_im * w_re], axis=1)
             )
-        half = from_right(jnp.concatenate(exits, axis=0), first_down[...])
-        stacked = jnp.concatenate(
-            [
-                jnp.concatenate(
-                    [half[m * window:(m + 1) * window, c * window:(c + 1) * window] for m in range(modes)],
-                    axis=1,
-                )
-                for c in range(2)
-            ],
-            axis=0,
-        )
-        field = from_left(second_across[...], stacked)
-        power = jnp.zeros((window, window), F32)
+        return exits
+
+    def scale_of(slot, blocks):
+        power = blocks[0][0] * blocks[0][0]
         for m in range(modes):
             for c in range(2):
-                piece = field[c * window:(c + 1) * window, m * window:(m + 1) * window]
-                power = power + piece * piece
+                if m or c:
+                    power = power + blocks[m][c] * blocks[m][c]
         amplitude = (received[slot, 0:window, :].astype(jnp.int32).astype(F32) + HALF) * (TOP / STEPS)
-        scaling = valid * (1.0 - amplitude * lax.rsqrt(jnp.maximum(power, 0.25)))
-        scaled = jnp.concatenate(
-            [
-                jnp.concatenate(
-                    [
-                        scaling * field[c * window:(c + 1) * window, m * window:(m + 1) * window]
-                        for c in range(2)
-                    ],
-                    axis=1,
-                )
-                for m in range(modes)
-            ],
-            axis=0,
-        )
-        half = from_right(scaled, second_down[...])
-        stacked = jnp.concatenate(
-            [
-                jnp.concatenate(
-                    [half[m * window:(m + 1) * window, c * window:(c + 1) * window] for m in range(modes)],
-                    axis=1,
-                )
-                for c in range(2)
-            ],
-            axis=0,
-        )
-        back = from_left(first_across[...], stacked)
+        return notes[slot, 2].astype(F32) * (1.0 - amplitude * lax.rsqrt(jnp.maximum(power, 0.25)))
+
+    def finish(slot, w_re, w_im, back):
+        start = jnp.clip(notes[slot, 1], 1, window - 1)
+        rows = pl.ds(notes[slot, 0], window)
         patch_re = jnp.zeros((window, window), F32)
         patch_im = jnp.zeros((window, window), F32)
         for m in range(modes):
             p_re, p_im = probe_full[m, 0], probe_full[m, 1]
-            b_re = back[0:window, m * window:(m + 1) * window]
-            b_im = back[window:, m * window:(m + 1) * window]
+            b_re, b_im = back[m]
             patch_re = patch_re + (p_re * b_re + p_im * b_im)
             patch_im = patch_im + (p_re * b_im - p_im * b_re)
             probe_total[2 * m] += w_re * b_re + w_im * b_im
@@ -168,12 +134,41 @@
             total[part, 0, rows, :] += jnp.where(lane >= start, turned, 0.0)
             total[part, 1, rows, :] += jnp.where(lane < start, turned, 0.0)
 
+    def several(slots_now):
+        cuts = [cut(slot) for slot in slots_now]
+        exits = [e for w in cuts for e in leave(*w)]
+        field = both_ways(exits, first_down[...], second_across[...])
+        scaled = []
+        for u, slot in enumerate(slots_now):
+            mine = field[u * modes:(u + 1) * modes]
+            scaling = scale_of(slot, mine)
+            scaled += [jnp.concatenate([scaling * b[0], scaling * b[1]], axis=1) for b in mine]
+        back = both_ways(scaled, second_down[...], first_across[...])
+        for u, slot in enumerate(slots_now):
+            finish(slot, *cuts[u], back[u * modes:(u + 1) * modes])
+
+    def both_ways(blocks, down, across):
+        count = len(blocks)
+        half = from_right(jnp.concatenate(blocks, axis=0), down)
+        pieces = [
+            [half[b * window:(b + 1) * window, c * window:(c + 1) * window] for c in range(2)]
+            for b in range(count)
+        ]
+        stacked = jnp.concatenate(
+            [jnp.concatenate([p[c] for p in pieces], axis=1) for c in range(2)], axis=0
+        )
+        out = from_left(across, stacked)
+        return [
+            [out[c * window:(c + 1) * window, b * window:(b + 1) * window] for c in range(2)]
+            for b in range(count)
+        ]
+
     def step(at, carry):
-        one(at)
+        several([GROUP * at + u for u in range(GROUP)])
         return carry
 
     shifts[...] = jnp.zeros(shifts.shape, F32)
-    lax.fori_loop(0, slots, step, 0)
+    lax.fori_loop(0, slots // GROUP, step, 0)
     deep = height // bands
     piece = 2 * modes * window // bands
     for b in range(bands):

time: 143 us -> 120 us (0.84)
  Pallas kernels: 34.2 us -> 13 us
    pallas_call x1, Pallas kernels: 32.5 us -> 11.3 us  [compute(): pl.pallas_call(main_kernel, grid=(1,), out_shape=(jax.ShapeDtypeStruct((b...]
  transfers between devices with their start and end apart: 5 -> 5, of which waited for: 3 -> 3; matrix products, arithmetic and copies ran while one was open for 2% -> 3% of each run, Pallas kernels for 0% -> 0%
where the time goes in v2:
time: 120 us
  waiting for transfers between devices  37.7 us (31%)
  blocking collectives  33.1 us (28%)
  starting transfers between devices  27.7 us (23%)
  Pallas kernels  13 us (11%)
  local copies, waits for them, and re-layouts  5.23 us (4%)
  other arithmetic  2.35 us (2%)
    all_to_all x3, waiting for transfers between devices, exchange(): return lax.all_to_all(value, axis, split_axis=0, concat_axis=0, tiled=True)  37.7 us
    all_to_all x1, blocking collectives, exchange(): return lax.all_to_all(value, axis, split_axis=0, concat_axis=0, tiled=True)  33.1 us
    all_to_all x3, starting transfers between devices, exchange(): return lax.all_to_all(value, axis, split_axis=0, concat_axis=0, tiled=True)  22.1 us
    pallas_call x1, Pallas kernels, compute(): pl.pallas_call(main_kernel, grid=(1,), out_shape=(jax.ShapeDtypeStruct((b...  11.3 us
    unnamed x19, local copies, waits for them, and re-layouts  3.69 us
    ppermute x1, starting transfers between devices, local(): lax.ppermute(strips[:, 1], 'tile', [(t, t + 1) for t in range(tiles - 1)])  3.54 us
  transfers between devices with their start and end apart: 5, of which 3 were waited for; matrix products, arithmetic and copies ran while one was open for 3% of the time, Pallas kernels for 0%

profile of v2, /device:TPU:1, one launch (start us, length us, event | category | flops | bytes accessed | tf_op | source)
XLA Modules:
  0.0 119.9 jit_solution(8207692217865220935)
XLA Ops:
  0.6 0.0 copy-start
  0.6 0.9 copy.29.positions
  1.5 1.0 copy-done.1
  2.6 1.7 %shard_map.103 = s16[16,144,128]{2,1,0:T(8,128)(2,1)} custom-call(s32[8,2]{1,0:T(8,128)S(1)} %copy.29.positions, f32[8,128,128]{2,1,0:T(8,128)S(1)} %copy-done.1), custom_call_target="tpu_custom_call" | custom-call | tf_op jit(solution)/shard_map/pallas_call | solution.py:192
  4.3 10.2 %all-to-all-start = ((s16[16,144,128]{2,1,0:T(8,128)(2,1)}), s16[16,144,128]{2,1,0:T(8,128)(2,1)S(1)}, u32[]{:S(2)}, u32[]{:S(2)}) async-start(s16[16,144,128]{2,1,0:T(8,128)(2,1)} %shard_map.103), calls=%async_computation | async-start | bytes 1179648 | tf_op jit(solution)/shard_map/all_to_all | solution.py:241
  14.6 0.0 copy-done
  14.6 0.7 slice.52
  15.3 2.1 %collective-permute-start = (bf16[2,512,128]{2,1,0:T(8,128)(2,1)}, bf16[2,512,128]{2,1,0:T(8,128)(2,1)S(1)}, u32[]{:S(2)}, u32[]{:S(2)}) collective-permute-start(bf16[2,512,128]{2,1,0:T(8,128)(2,1)} %slice.52), channel_id=1, source_target_pairs={{1,0},{2,1},{3,2},{4,3},{5,4},{6,5},{7,6},{8,7},{9,8},{10,9},{11,1... | collective-permute-start | bytes 786440 | tf_op jit(solution)/shard_map/ppermute | solution.py:253
  17.4 15.8 %all-to-all-done.received = s16[16,144,128]{2,1,0:T(8,128)(2,1)S(1)} async-done(((s16[16,144,128]{2,1,0:T(8,128)(2,1)}), s16[16,144,128]{2,1,0:T(8,128)(2,1)S(1)}, u32[]{:S(2)}, u32[]{:S(2)}) %all-to-all-start) | async-done | bytes 589856 | tf_op jit(solution)/shard_map/all_to_all | solution.py:241
  33.2 0.0 collective-permute-done.margin
  33.2 0.0 copy-done.2
  33.2 0.0 copy-done.3
  33.3 0.0 copy-start.6
  33.3 0.9 copy-done.6
  34.2 11.3 %shard_map.104 = (bf16[32,96,128]{2,1,0:T(8,128)(2,1)S(1)}, f32[16,8,128]{2,1,0:T(8,128)S(1)}) custom-call(s32[16,3]{1,0:T(8,128)S(1)} %bitcast.11, s16[16,144,128]{2,1,0:T(8,128)(2,1)S(1)} %all-to-all-done.received, f32[2,512,384]{2,1,0:T(8,128)S(1)} %copy-done, bf16[2,512,128]{2,1,0:T(8,128)(2,1)S(1)} %collective-permute-done.margin, ...), custom_call_target="tpu_custom_call" | custom-call | tf_op jit(solution)/shard_map/pallas_call | solution.py:215
  45.5 0.0 copy-start.7
  45.5 33.1 %all_to_all.20 = bf16[32,96,128]{2,1,0:T(8,128)(2,1)S(1)} all-to-all(bf16[32,96,128]{2,1,0:T(8,128)(2,1)S(1)} %get-tuple-element.5), channel_id=1, replica_groups=mesh['scan'=32,'tile'=16] {'scan'}, dimensions={0} | all-to-all | bytes 1572864 | tf_op jit(solution)/shard_map/all_to_all | solution.py:241
  78.6 0.1 convert_reduce_fusion
  78.7 0.7 pad_maximum_fusion
  79.5 6.6 %all-to-all-start.2 = ((f32[16,32,128]{2,1,0:T(8,128)}), f32[16,32,128]{2,1,0:T(8,128)S(1)}, u32[]{:S(2)}, u32[]{:S(2)}) async-start(f32[16,32,128]{2,1,0:T(8,128)} %pad_maximum_fusion), calls=%async_computation.2 | async-start | bytes 524288 | tf_op jit(solution)/shard_map/all_to_all | solution.py:241
  86.1 3.5 %collective-permute-start.1 = (f32[2,16,128]{2,1,0:T(8,128)S(1)}, f32[2,16,128]{2,1,0:T(8,128)S(1)}, u32[]{:S(2)}, u32[]{:S(2)}) collective-permute-start(f32[2,16,128]{2,1,0:T(8,128)S(1)} %get-tuple-element.7), channel_id=1, source_target_pairs={{0,1},{1,2},{2,3},{3,4},{4,5},{5,6},{6,7},{7,8},{8,9},{9,10},{10,1... | collective-permute-start | bytes 49160 | tf_op jit(solution)/shard_map/ppermute | solution.py:261
  89.6 8.4 %all-to-all-done.2 = f32[16,32,128]{2,1,0:T(8,128)S(1)} async-done(((f32[16,32,128]{2,1,0:T(8,128)}), f32[16,32,128]{2,1,0:T(8,128)S(1)}, u32[]{:S(2)}, u32[]{:S(2)}) %all-to-all-start.2) | async-done | bytes 262176 | tf_op jit(solution)/shard_map/all_to_all | solution.py:241
  98.0 0.8 broadcast_in_dim.41
  98.8 5.2 %all-to-all-start.3 = ((f32[32,24,128]{2,1,0:T(8,128)}), f32[32,24,128]{2,1,0:T(8,128)S(1)}, u32[]{:S(2)}, u32[]{:S(2)}) async-start(f32[32,24,128]{2,1,0:T(8,128)} %broadcast_in_dim.41), calls=%async_computation.3 | async-start | bytes 786432 | tf_op jit(solution)/shard_map/all_to_all | solution.py:241
  104.0 0.1 iota_compare_fusion
  104.1 0.0 collective-permute-done.1
  104.1 0.6 pad_maximum_fusion.1
  104.7 0.1 slice_reduce_fusion.1
  104.8 0.1 copy.35
  104.9 0.7 select_reduce_fusion
  105.6 13.6 %all-to-all-done.3 = f32[32,24,128]{2,1,0:T(8,128)S(1)} async-done(((f32[32,24,128]{2,1,0:T(8,128)}), f32[32,24,128]{2,1,0:T(8,128)S(1)}, u32[]{:S(2)}, u32[]{:S(2)}) %all-to-all-start.3) | async-done | bytes 393248 | tf_op jit(solution)/shard_map/all_to_all | solution.py:241
  119.2 0.7 copy.38
  (19 shorter events, 0.1 us)
Async XLA Ops:
  0.6 13.9 %copy-start = (f32[2,512,384]{2,1,0:T(8,128)S(1)}, f32[2,512,384]{2,1,0:T(8,128)}, u32[]{:S(2)}) copy-start(f32[2,512,384]{2,1,0:T(8,128)} %own.1) | copy-start | bytes 4718596
  1.5 1.0 copy-start.1
  2.6 30.7 %copy-start.2 = (bf16[512,256]{1,0:T(8,128)(2,1)S(1)}, bf16[512,256]{1,0:T(8,128)(2,1)}, u32[]{:S(2)}) copy-start(bf16[512,256]{1,0:T(8,128)(2,1)} %constant.28.clone.first_down) | copy-start | bytes 786436
  2.6 30.7 %copy-start.3 = (bf16[256,512]{1,0:T(8,128)(2,1)S(1)}, bf16[256,512]{1,0:T(8,128)(2,1)}, u32[]{:S(2)}) copy-start(bf16[256,512]{1,0:T(8,128)(2,1)} %constant.29.clone.first_across) | copy-start | bytes 786436
  2.6 30.7 %copy-start.4 = (bf16[512,256]{1,0:T(8,128)(2,1)S(1)}, bf16[512,256]{1,0:T(8,128)(2,1)}, u32[]{:S(2)}) copy-start(bf16[512,256]{1,0:T(8,128)(2,1)} %constant.30.clone.second_down) | copy-start | bytes 786436
  2.6 30.7 %copy-start.5 = (bf16[256,512]{1,0:T(8,128)(2,1)S(1)}, bf16[256,512]{1,0:T(8,128)(2,1)}, u32[]{:S(2)}) copy-start(bf16[256,512]{1,0:T(8,128)(2,1)} %constant.31.clone.second_across) | copy-start | bytes 786436
  4.3 28.9 %all-to-all-start = ((s16[16,144,128]{2,1,0:T(8,128)(2,1)}), s16[16,144,128]{2,1,0:T(8,128)(2,1)S(1)}, u32[]{:S(2)}, u32[]{:S(2)}) async-start(s16[16,144,128]{2,1,0:T(8,128)(2,1)} %shard_map.103), calls=%async_computation | async-start | bytes 1179648 | tf_op jit(solution)/shard_map/all_to_all | solution.py:241
  15.3 17.9 %collective-permute-start = (bf16[2,512,128]{2,1,0:T(8,128)(2,1)}, bf16[2,512,128]{2,1,0:T(8,128)(2,1)S(1)}, u32[]{:S(2)}, u32[]{:S(2)}) collective-permute-start(bf16[2,512,128]{2,1,0:T(8,128)(2,1)} %slice.52), channel_id=1, source_target_pairs={{1,0},{2,1},{3,2},{4,3},{5,4},{6,5},{7,6},{8,7},{9,8},{10,9},{11,1... | collective-permute-start | bytes 786440 | tf_op jit(solution)/shard_map/ppermute | solution.py:253
  33.3 0.9 copy-start.6
  45.5 40.6 %copy-start.7 = (s32[8,2]{0,1:T(2,128)S(1)}, s32[8,2]{0,1:T(2,128)}, u32[]{:S(2)}) copy-start(s32[8,2]{0,1:T(2,128)} %param.11) | copy-start | bytes 196
  79.5 18.5 %all-to-all-start.2 = ((f32[16,32,128]{2,1,0:T(8,128)}), f32[16,32,128]{2,1,0:T(8,128)S(1)}, u32[]{:S(2)}, u32[]{:S(2)}) async-start(f32[16,32,128]{2,1,0:T(8,128)} %pad_maximum_fusion), calls=%async_computation.2 | async-start | bytes 524288 | tf_op jit(solution)/shard_map/all_to_all | solution.py:241
  86.1 18.0 %collective-permute-start.1 = (f32[2,16,128]{2,1,0:T(8,128)S(1)}, f32[2,16,128]{2,1,0:T(8,128)S(1)}, u32[]{:S(2)}, u32[]{:S(2)}) collective-permute-start(f32[2,16,128]{2,1,0:T(8,128)S(1)} %get-tuple-element.7), channel_id=1, source_target_pairs={{0,1},{1,2},{2,3},{3,4},{4,5},{5,6},{6,7},{7,8},{8,9},{9,10},{10,1... | collective-permute-start | bytes 49160 | tf_op jit(solution)/shard_map/ppermute | solution.py:261
  98.8 20.4 %all-to-all-start.3 = ((f32[32,24,128]{2,1,0:T(8,128)}), f32[32,24,128]{2,1,0:T(8,128)S(1)}, u32[]{:S(2)}, u32[]{:S(2)}) async-start(f32[32,24,128]{2,1,0:T(8,128)} %broadcast_in_dim.41), calls=%async_computation.3 | async-start | bytes 786432 | tf_op jit(solution)/shard_map/all_to_all | solution.py:241

commit v3 on v2

--- a/solution.py
+++ b/solution.py
@@ -45,6 +45,18 @@
 def from_left(table, value):
     high = value.astype(BF16)
     return jnp.dot(table, jnp.concatenate([high, high], axis=0), preferred_element_type=F32)
+
+
+STEP_MASKS = (1, 8, 24, 2, 4)
+
+
+def step_bits(scan):
+    return (scan & 1, (scan >> 3 ^ scan >> 4) & 1, scan >> 4 & 1, scan >> 1 & 1, scan >> 2 & 1)
+
+
+def pair_order(bands):
+    even = [scan for scan in range(bands) if scan % 2 == 0]
+    return sorted(even, key=step_bits)
 
 
 def pack_kernel(positions, measured, packed):
@@ -66,12 +78,12 @@
 
 def main_kernel(
     notes, received, own, margin, probe, first_down, first_across, second_down, second_across,
-    sums, shifts, strip, total, probe_total, probe_full,
+    probe_sums, keep, give, shifts, strip, total, probe_total, probe_full,
 ):
     slots = received.shape[0]
     modes = probe.shape[0]
     window = probe.shape[2]
-    bands = sums.shape[0]
+    bands = probe_sums.shape[0]
     height = own.shape[1]
     for part in range(2):
         strip[part, 0] = own[part].astype(BF16).astype(F32)
@@ -169,13 +181,16 @@
 
     shifts[...] = jnp.zeros(shifts.shape, F32)
     lax.fori_loop(0, slots // GROUP, step, 0)
+    mine = lax.axis_index("scan") & 1
     deep = height // bands
+    for at, band in enumerate(pair_order(bands)):
+        for part in range(2):
+            for side in range(2):
+                for out, who in ((keep, mine), (give, 1 - mine)):
+                    start = pl.multiple_of((band + who) * deep, deep)
+                    out[at, part, side] = total[part, side, pl.ds(start, deep), :].astype(out.dtype)
     piece = 2 * modes * window // bands
     for b in range(bands):
-        for part in range(2):
-            for side in range(2):
-                at = (2 * part + side) * deep
-                sums[b, at:at + deep, :] = total[part, side, b * deep:(b + 1) * deep, :].astype(BF16)
         mode, offset = divmod(b * piece, window)
         parts = []
         left = piece
@@ -183,8 +198,8 @@
             take = min(left, window - offset)
             parts.append(probe_total[mode, offset:offset + take, :])
             mode, offset, left = mode + 1, 0, left - take
-        parts.append(jnp.zeros((sums.shape[1] - 4 * deep - piece, window), F32))
-        sums[b, 4 * deep:, :] = jnp.concatenate(parts, axis=0).astype(BF16)
+        parts.append(jnp.zeros((probe_sums.shape[1] - piece, window), F32))
+        probe_sums[b] = jnp.concatenate(parts, axis=0).astype(BF16)
 
 
 def pack(positions, measured, slots):
@@ -211,12 +226,15 @@
     def whole(shape):
         return pl.BlockSpec(shape, lambda i: (0,) * len(shape))
 
-    rows = 4 * (height // bands) + -(-(2 * modes * window // bands) // 16) * 16
+    rows = -(-(2 * modes * window // bands) // 16) * 16
+    half = (bands // 2, 2, 2, height // bands, window)
     return pl.pallas_call(
         main_kernel,
         grid=(1,),
         out_shape=(
             jax.ShapeDtypeStruct((bands, rows, window), BF16),
+            jax.ShapeDtypeStruct(half, F32),
+            jax.ShapeDtypeStruct(half, BF16),
             jax.ShapeDtypeStruct((slots, 8, window), F32),
         ),
         in_specs=[
@@ -226,7 +244,7 @@
             whole(margin.shape),
             whole(probe.shape),
         ] + [whole(table.shape) for table in tables],
-        out_specs=(whole((bands, rows, window)), whole((slots, 8, window))),
+        out_specs=(whole((bands, rows, window)), whole(half), whole(half), whole((slots, 8, window))),
         scratch_shapes=[
             pltpu.VMEM((2, 2, height, window), F32),
             pltpu.VMEM((2, 2, height, window), F32),
@@ -255,14 +273,25 @@
     )
     received = exchange(pack(positions, measured, tiles), "tile")
     notes = received[:, window, :3].astype(jnp.int32)
-    sums, shifts = compute(notes, received, object_field, margin, probe, bands)
-    gathered = jnp.sum(exchange(sums, "scan").astype(F32), axis=0)
-    strips = gathered[:4 * deep].reshape(2, 2, deep, window)
+    probe_sums, keep, give, shifts = compute(notes, received, object_field, margin, probe, bands)
+    bits = step_bits(lax.axis_index("scan"))
+    for at, mask in enumerate(STEP_MASKS):
+        pairs = [(scan, scan ^ mask) for scan in range(bands)]
+        current = keep + lax.ppermute(give, "scan", pairs).astype(F32)
+        if at + 1 < len(STEP_MASKS):
+            half = current.shape[0] // 2
+            upper = bits[at + 1] == 1
+            keep = jnp.where(upper, current[half:], current[:half])
+            give = jnp.where(upper, current[:half], current[half:])
+            if at == 0:
+                give = give.astype(BF16)
+    strips = current[0]
+    gathered = jnp.sum(exchange(probe_sums, "scan").astype(F32), axis=0)
     spilled = lax.ppermute(strips[:, 1], "tile", [(t, t + 1) for t in range(tiles - 1)])
     object_grad = jnp.concatenate(
         [spilled, jnp.zeros((2, deep, width - 2 * window), F32), strips[:, 0]], axis=2
     )
-    own_piece = gathered[4 * deep:4 * deep + piece]
+    own_piece = gathered[:piece]
     outgoing = jnp.concatenate(
         [jnp.broadcast_to(own_piece[None], (tiles, piece, window)), shifts], axis=1
     )

time: 120 us -> 135 us (1.12)
  starting transfers between devices: 27.7 us -> 62.9 us
  blocking collectives: 33.1 us -> 0 us
  waiting for transfers between devices: 37.7 us -> 46.9 us
  local copies, waits for them, and re-layouts: 5.23 us -> 7.12 us
    all_to_all x1 -> x0, blocking collectives: 33.1 us -> none  [exchange(): return lax.all_to_all(value, axis, split_axis=0, concat_axis=0, tiled=True)]
    ppermute x0 -> x5, starting transfers between devices: none -> 20.9 us  [local(): current = keep + lax.ppermute(give, 'scan', pairs).astype(F32)]
    all_to_all x3 -> x4, starting transfers between devices: 22.1 us -> 35.8 us  [exchange(): return lax.all_to_all(value, axis, split_axis=0, concat_axis=0, tiled=True)]
    ppermute x0 -> x5, waiting for transfers between devices: none -> 9.26 us  [local(): current = keep + lax.ppermute(give, 'scan', pairs).astype(F32)]
    unnamed x19 -> x23, local copies, waits for them, and re-layouts: 3.69 us -> 6.28 us
    all_to_all x3 -> x4, waiting for transfers between devices: 37.7 us -> 37.6 us  [exchange(): return lax.all_to_all(value, axis, split_axis=0, concat_axis=0, tiled=True)]
  transfers between devices with their start and end apart: 5 -> 11, of which waited for: 3 -> 7; matrix products, arithmetic and copies ran while one was open for 3% -> 2% of each run, Pallas kernels for 0% -> 0%
where the time goes in v3:
time: 135 us; the launch traced here: 134 us
  starting transfers between devices  62.9 us (47%)
  waiting for transfers between devices  46.9 us (35%)
  Pallas kernels  13.9 us (10%)
  local copies, waits for them, and re-layouts  7.12 us (5%)
  other arithmetic  2.53 us (2%)
    all_to_all x4, waiting for transfers between devices, exchange(): return lax.all_to_all(value, axis, split_axis=0, concat_axis=0, tiled=True)  37.6 us
    all_to_all x4, starting transfers between devices, exchange(): return lax.all_to_all(value, axis, split_axis=0, concat_axis=0, tiled=True)  35.8 us
    ppermute x5, starting transfers between devices, local(): current = keep + lax.ppermute(give, 'scan', pairs).astype(F32)  20.9 us
    pallas_call x1, Pallas kernels, compute(): pl.pallas_call(main_kernel, grid=(1,), out_shape=(jax.ShapeDtypeStruct((b...  12.2 us
    ppermute x5, waiting for transfers between devices, local(): current = keep + lax.ppermute(give, 'scan', pairs).astype(F32)  9.26 us
    unnamed x23, local copies, waits for them, and re-layouts  6.28 us
    ppermute x1, starting transfers between devices, local(): lax.ppermute(strips[:, 1], 'tile', [(t, t + 1) for t in range(tiles - 1)])  4.05 us
  transfers between devices with their start and end apart: 11, of which 7 were waited for; matrix products, arithmetic and copies ran while one was open for 2% of the time, Pallas kernels for 0%

profile of v3, /device:TPU:1, one launch (start us, length us, event | category | flops | bytes accessed | tf_op | source)
XLA Modules:
  0.0 134.3 jit_solution(14244664694290527220)
XLA Ops:
  0.6 0.9 copy.26.positions
  1.5 1.0 copy-done.1
  2.6 1.7 %shard_map.103 = s16[16,144,128]{2,1,0:T(8,128)(2,1)} custom-call(s32[8,2]{1,0:T(8,128)S(1)} %copy.26.positions, f32[8,128,128]{2,1,0:T(8,128)S(1)} %copy-done.1), custom_call_target="tpu_custom_call" | custom-call | tf_op jit(solution)/shard_map/pallas_call | solution.py:207
  4.3 10.2 %all-to-all-start = ((s16[16,144,128]{2,1,0:T(8,128)(2,1)}), s16[16,144,128]{2,1,0:T(8,128)(2,1)S(1)}, u32[]{:S(2)}, u32[]{:S(2)}) async-start(s16[16,144,128]{2,1,0:T(8,128)(2,1)} %shard_map.103), calls=%async_computation | async-start | bytes 1179648 | tf_op jit(solution)/shard_map/all_to_all | solution.py:259
  14.6 2.1 %collective-permute-start = (bf16[2,512,128]{2,1,0:T(8,128)(2,1)S(1)}, bf16[2,512,128]{2,1,0:T(8,128)(2,1)S(1)}, u32[]{:S(2)}, u32[]{:S(2)}) collective-permute-start(bf16[2,512,128]{2,1,0:T(8,128)(2,1)S(1)} %slice.111), channel_id=1, source_target_pairs={{1,0},{2,1},{3,2},{4,3},{5,4},{6,5},{7,6},{8,7},{9,8},{10,9},{11,1... | collective-permute-start | bytes 786440 | tf_op jit(solution)/shard_map/ppermute | solution.py:271
  16.7 16.5 %all-to-all-done.received = s16[16,144,128]{2,1,0:T(8,128)(2,1)S(1)} async-done(((s16[16,144,128]{2,1,0:T(8,128)(2,1)}), s16[16,144,128]{2,1,0:T(8,128)(2,1)S(1)}, u32[]{:S(2)}, u32[]{:S(2)}) %all-to-all-start) | async-done | bytes 589856 | tf_op jit(solution)/shard_map/all_to_all | solution.py:259
  33.2 0.7 copy-done.6
  33.9 0.9 copy-done.5
  34.9 0.9 copy-done.7
  35.8 0.9 copy-done.8
  36.8 12.2 %shard_map.104 = (bf16[32,32,128]{2,1,0:T(8,128)(2,1)}, f32[16,2,2,16,128]{4,3,2,1,0:T(8,128)S(1)}, bf16[16,2,2,16,128]{4,3,2,1,0:T(8,128)(2,1)}, f32[16,8,128]{2,1,0:T(8,128)S(1)}) custom-call(s32[16,3]{1,0:T(8,128)S(1)} %bitcast.12, s16[16,144,128]{2,1,0:T(8,128)(2,1)S(1)} %all-to-all-done.received, f32[2,512,384]{2,1,0:T(8,128)S(1)} %copy-done, ...), custom_call_target="tpu_custom_call" | custom-call | tf_op jit(solution)/shard_map/pallas_call | solution.py:231
  48.9 1.9 %collective-permute-start.1 = (bf16[16,2,2,16,128]{4,3,2,1,0:T(8,128)(2,1)}, bf16[16,2,2,16,128]{4,3,2,1,0:T(8,128)(2,1)S(1)}, u32[]{:S(2)}, u32[]{:S(2)}) collective-permute-start(bf16[16,2,2,16,128]{4,3,2,1,0:T(8,128)(2,1)} %get-tuple-element.8), channel_id=1, source_target_pairs={{0,16},{16,0},{32,48},{48,32},{64,80},{80,64},{96,112},{112,96},{1... | collective-permute-start | bytes 786440 | tf_op jit(solution)/shard_map/ppermute | solution.py:280
  50.9 7.3 %collective-permute-done.1 = bf16[16,2,2,16,128]{4,3,2,1,0:T(8,128)(2,1)S(1)} collective-permute-done((bf16[16,2,2,16,128]{4,3,2,1,0:T(8,128)(2,1)}, bf16[16,2,2,16,128]{4,3,2,1,0:T(8,128)(2,1)S(1)}, u32[]{:S(2)}, u32[]{:S(2)}) %collective-permute-start.1) | collective-permute-done | bytes 262176 | tf_op jit(solution)/shard_map/ppermute | solution.py:280
  58.3 4.1 %collective-permute-start.2 = (bf16[8,2,2,16,128]{4,3,2,1,0:T(8,128)(2,1)S(1)}, bf16[8,2,2,16,128]{4,3,2,1,0:T(8,128)(2,1)S(1)}, u32[]{:S(2)}, u32[]{:S(2)}) collective-permute-start(bf16[8,2,2,16,128]{4,3,2,1,0:T(8,128)(2,1)S(1)} %select_convert_fusion), channel_id=1, source_target_pairs={{0,128},{16,144},{32,160},{48,176},{64,192},{80,208},{96,224},{112... | collective-permute-start | bytes 393224 | tf_op jit(solution)/shard_map/ppermute | solution.py:280
  62.4 11.0 %all-to-all-start.1 = ((bf16[32,32,128]{2,1,0:T(8,128)(2,1)}), bf16[32,32,128]{2,1,0:T(8,128)(2,1)S(1)}, u32[]{:S(2)}, u32[]{:S(2)}) async-start(bf16[32,32,128]{2,1,0:T(8,128)(2,1)} %get-tuple-element.9), calls=%async_computation.1 | async-start | bytes 524288 | tf_op jit(solution)/shard_map/all_to_all | solution.py:259
  73.6 5.3 %collective-permute-start.3 = (f32[4,2,2,16,128]{4,3,2,1,0:T(8,128)S(1)}, f32[4,2,2,16,128]{4,3,2,1,0:T(8,128)S(1)}, u32[]{:S(2)}, u32[]{:S(2)}) collective-permute-start(f32[4,2,2,16,128]{4,3,2,1,0:T(8,128)S(1)} %slice_select_fusion), channel_id=1, source_target_pairs={{0,384},{16,400},{32,416},{48,432},{64,448},{80,464},{96,480},{112... | collective-permute-start | bytes 393224 | tf_op jit(solution)/shard_map/ppermute | solution.py:280
  78.9 6.7 %all-to-all-done.1 = bf16[32,32,128]{2,1,0:T(8,128)(2,1)S(1)} async-done(((bf16[32,32,128]{2,1,0:T(8,128)(2,1)}), bf16[32,32,128]{2,1,0:T(8,128)(2,1)S(1)}, u32[]{:S(2)}, u32[]{:S(2)}) %all-to-all-start.1) | async-done | bytes 262176 | tf_op jit(solution)/shard_map/all_to_all | solution.py:259
  85.6 0.3 collective-permute-done.3
  86.0 4.6 %collective-permute-start.4 = (f32[2,2,2,16,128]{4,3,2,1,0:T(8,128)S(1)}, f32[2,2,2,16,128]{4,3,2,1,0:T(8,128)S(1)}, u32[]{:S(2)}, u32[]{:S(2)}) collective-permute-start(f32[2,2,2,16,128]{4,3,2,1,0:T(8,128)S(1)} %slice_select_fusion.1), channel_id=1, source_target_pairs={{0,32},{16,48},{32,0},{48,16},{64,96},{80,112},{96,64},{112,80},{1... | collective-permute-start | bytes 196616 | tf_op jit(solution)/shard_map/ppermute | solution.py:280
  90.7 0.7 pad_maximum_fusion
  91.4 7.4 %all-to-all-start.2 = ((f32[16,32,128]{2,1,0:T(8,128)}), f32[16,32,128]{2,1,0:T(8,128)S(1)}, u32[]{:S(2)}, u32[]{:S(2)}) async-start(f32[16,32,128]{2,1,0:T(8,128)} %pad_maximum_fusion), calls=%async_computation.2 | async-start | bytes 524288 | tf_op jit(solution)/shard_map/all_to_all | solution.py:259
  98.8 5.1 %collective-permute-start.5 = (f32[1,2,2,16,128]{4,3,2,1,0:T(8,128)S(1)}, f32[1,2,2,16,128]{4,3,2,1,0:T(8,128)S(1)}, u32[]{:S(2)}, u32[]{:S(2)}) collective-permute-start(f32[1,2,2,16,128]{4,3,2,1,0:T(8,128)S(1)} %slice_select_fusion.2), channel_id=1, source_target_pairs={{0,64},{16,80},{32,96},{48,112},{64,0},{80,16},{96,32},{112,48},{1... | collective-permute-start | bytes 98312 | tf_op jit(solution)/shard_map/ppermute | solution.py:280
  103.9 1.6 %collective-permute-done.5 = f32[1,2,2,16,128]{4,3,2,1,0:T(8,128)S(1)} collective-permute-done((f32[1,2,2,16,128]{4,3,2,1,0:T(8,128)S(1)}, f32[1,2,2,16,128]{4,3,2,1,0:T(8,128)S(1)}, u32[]{:S(2)}, u32[]{:S(2)}) %collective-permute-start.5) | collective-permute-done | bytes 32800 | tf_op jit(solution)/shard_map/ppermute | solution.py:280
  105.5 4.0 %collective-permute-start.6 = (f32[2,16,128]{2,1,0:T(8,128)S(1)}, f32[2,16,128]{2,1,0:T(8,128)S(1)}, u32[]{:S(2)}, u32[]{:S(2)}) collective-permute-start(f32[2,16,128]{2,1,0:T(8,128)S(1)} %get-tuple-element.11), channel_id=1, source_target_pairs={{0,1},{1,2},{2,3},{3,4},{4,5},{5,6},{6,7},{7,8},{8,9},{9,10},{10,1... | collective-permute-start | bytes 49160 | tf_op jit(solution)/shard_map/ppermute | solution.py:290
  109.6 0.9 all-to-all-done.2
  110.5 0.8 broadcast_in_dim.41
  111.3 7.1 %all-to-all-start.3 = ((f32[32,24,128]{2,1,0:T(8,128)}), f32[32,24,128]{2,1,0:T(8,128)S(1)}, u32[]{:S(2)}, u32[]{:S(2)}) async-start(f32[32,24,128]{2,1,0:T(8,128)} %broadcast_in_dim.41), calls=%async_computation.3 | async-start | bytes 786432 | tf_op jit(solution)/shard_map/all_to_all | solution.py:259
  118.5 0.6 pad_maximum_fusion.1
  119.1 0.1 slice_reduce_fusion.1
  119.3 0.7 select_reduce_fusion
  119.9 13.6 %all-to-all-done.3 = f32[32,24,128]{2,1,0:T(8,128)S(1)} async-done(((f32[32,24,128]{2,1,0:T(8,128)}), f32[32,24,128]{2,1,0:T(8,128)S(1)}, u32[]{:S(2)}, u32[]{:S(2)}) %all-to-all-start.3) | async-done | bytes 393248 | tf_op jit(solution)/shard_map/all_to_all | solution.py:259
  133.5 0.7 copy.35
  (42 shorter events, 0.6 us)
Async XLA Ops:
  0.6 13.9 %copy-start = (f32[2,512,384]{2,1,0:T(8,128)S(1)}, f32[2,512,384]{2,1,0:T(8,128)}, u32[]{:S(2)}) copy-start(f32[2,512,384]{2,1,0:T(8,128)} %own.1) | copy-start | bytes 4718596
  1.5 1.0 copy-start.1
  2.6 31.4 %copy-start.2 = (bf16[512,256]{1,0:T(8,128)(2,1)S(1)}, bf16[512,256]{1,0:T(8,128)(2,1)}, u32[]{:S(2)}) copy-start(bf16[512,256]{1,0:T(8,128)(2,1)} %constant.41.clone.first_down) | copy-start | bytes 786436
  2.6 31.4 %copy-start.3 = (bf16[256,512]{1,0:T(8,128)(2,1)S(1)}, bf16[256,512]{1,0:T(8,128)(2,1)}, u32[]{:S(2)}) copy-start(bf16[256,512]{1,0:T(8,128)(2,1)} %constant.42.clone.first_across) | copy-start | bytes 786436
  2.6 31.4 %copy-start.4 = (bf16[512,256]{1,0:T(8,128)(2,1)S(1)}, bf16[512,256]{1,0:T(8,128)(2,1)}, u32[]{:S(2)}) copy-start(bf16[512,256]{1,0:T(8,128)(2,1)} %constant.43.clone.second_down) | copy-start | bytes 786436
  4.3 28.9 %all-to-all-start = ((s16[16,144,128]{2,1,0:T(8,128)(2,1)}), s16[16,144,128]{2,1,0:T(8,128)(2,1)S(1)}, u32[]{:S(2)}, u32[]{:S(2)}) async-start(s16[16,144,128]{2,1,0:T(8,128)(2,1)} %shard_map.103), calls=%async_computation | async-start | bytes 1179648 | tf_op jit(solution)/shard_map/all_to_all | solution.py:259
  14.6 18.6 %collective-permute-start = (bf16[2,512,128]{2,1,0:T(8,128)(2,1)S(1)}, bf16[2,512,128]{2,1,0:T(8,128)(2,1)S(1)}, u32[]{:S(2)}, u32[]{:S(2)}) collective-permute-start(bf16[2,512,128]{2,1,0:T(8,128)(2,1)S(1)} %slice.111), channel_id=1, source_target_pairs={{1,0},{2,1},{3,2},{4,3},{5,4},{6,5},{7,6},{8,7},{9,8},{10,9},{11,1... | collective-permute-start | bytes 786440 | tf_op jit(solution)/shard_map/ppermute | solution.py:271
  33.2 0.7 copy-start.6
  33.9 1.0 copy-start.5
  34.9 0.9 copy-start.7
  35.8 0.9 copy-start.8
  48.9 9.2 %collective-permute-start.1 = (bf16[16,2,2,16,128]{4,3,2,1,0:T(8,128)(2,1)}, bf16[16,2,2,16,128]{4,3,2,1,0:T(8,128)(2,1)S(1)}, u32[]{:S(2)}, u32[]{:S(2)}) collective-permute-start(bf16[16,2,2,16,128]{4,3,2,1,0:T(8,128)(2,1)} %get-tuple-element.8), channel_id=1, source_target_pairs={{0,16},{16,0},{32,48},{48,32},{64,80},{80,64},{96,112},{112,96},{1... | collective-permute-start | bytes 786440 | tf_op jit(solution)/shard_map/ppermute | solution.py:280
  58.3 15.2 %collective-permute-start.2 = (bf16[8,2,2,16,128]{4,3,2,1,0:T(8,128)(2,1)S(1)}, bf16[8,2,2,16,128]{4,3,2,1,0:T(8,128)(2,1)S(1)}, u32[]{:S(2)}, u32[]{:S(2)}) collective-permute-start(bf16[8,2,2,16,128]{4,3,2,1,0:T(8,128)(2,1)S(1)} %select_convert_fusion), channel_id=1, source_target_pairs={{0,128},{16,144},{32,160},{48,176},{64,192},{80,208},{96,224},{112... | collective-permute-start | bytes 393224 | tf_op jit(solution)/shard_map/ppermute | solution.py:280
  62.4 23.2 %all-to-all-start.1 = ((bf16[32,32,128]{2,1,0:T(8,128)(2,1)}), bf16[32,32,128]{2,1,0:T(8,128)(2,1)S(1)}, u32[]{:S(2)}, u32[]{:S(2)}) async-start(bf16[32,32,128]{2,1,0:T(8,128)(2,1)} %get-tuple-element.9), calls=%async_computation.1 | async-start | bytes 524288 | tf_op jit(solution)/shard_map/all_to_all | solution.py:259
  73.5 30.3 %copy-start.9 = (s32[8,2]{0,1:T(2,128)S(1)}, s32[8,2]{0,1:T(2,128)}, u32[]{:S(2)}) copy-start(s32[8,2]{0,1:T(2,128)} %param.11) | copy-start | bytes 196
  73.6 12.4 %collective-permute-start.3 = (f32[4,2,2,16,128]{4,3,2,1,0:T(8,128)S(1)}, f32[4,2,2,16,128]{4,3,2,1,0:T(8,128)S(1)}, u32[]{:S(2)}, u32[]{:S(2)}) collective-permute-start(f32[4,2,2,16,128]{4,3,2,1,0:T(8,128)S(1)} %slice_select_fusion), channel_id=1, source_target_pairs={{0,384},{16,400},{32,416},{48,432},{64,448},{80,464},{96,480},{112... | collective-permute-start | bytes 393224 | tf_op jit(solution)/shard_map/ppermute | solution.py:280
  86.0 12.7 %collective-permute-start.4 = (f32[2,2,2,16,128]{4,3,2,1,0:T(8,128)S(1)}, f32[2,2,2,16,128]{4,3,2,1,0:T(8,128)S(1)}, u32[]{:S(2)}, u32[]{:S(2)}) collective-permute-start(f32[2,2,2,16,128]{4,3,2,1,0:T(8,128)S(1)} %slice_select_fusion.1), channel_id=1, source_target_pairs={{0,32},{16,48},{32,0},{48,16},{64,96},{80,112},{96,64},{112,80},{1... | collective-permute-start | bytes 196616 | tf_op jit(solution)/shard_map/ppermute | solution.py:280
  91.4 19.1 %all-to-all-start.2 = ((f32[16,32,128]{2,1,0:T(8,128)}), f32[16,32,128]{2,1,0:T(8,128)S(1)}, u32[]{:S(2)}, u32[]{:S(2)}) async-start(f32[16,32,128]{2,1,0:T(8,128)} %pad_maximum_fusion), calls=%async_computation.2 | async-start | bytes 524288 | tf_op jit(solution)/shard_map/all_to_all | solution.py:259
  98.8 6.7 %collective-permute-start.5 = (f32[1,2,2,16,128]{4,3,2,1,0:T(8,128)S(1)}, f32[1,2,2,16,128]{4,3,2,1,0:T(8,128)S(1)}, u32[]{:S(2)}, u32[]{:S(2)}) collective-permute-start(f32[1,2,2,16,128]{4,3,2,1,0:T(8,128)S(1)} %slice_select_fusion.2), channel_id=1, source_target_pairs={{0,64},{16,80},{32,96},{48,112},{64,0},{80,16},{96,32},{112,48},{1... | collective-permute-start | bytes 98312 | tf_op jit(solution)/shard_map/ppermute | solution.py:280
  105.5 13.0 %collective-permute-start.6 = (f32[2,16,128]{2,1,0:T(8,128)S(1)}, f32[2,16,128]{2,1,0:T(8,128)S(1)}, u32[]{:S(2)}, u32[]{:S(2)}) collective-permute-start(f32[2,16,128]{2,1,0:T(8,128)S(1)} %get-tuple-element.11), channel_id=1, source_target_pairs={{0,1},{1,2},{2,3},{3,4},{4,5},{5,6},{6,7},{7,8},{8,9},{9,10},{10,1... | collective-permute-start | bytes 49160 | tf_op jit(solution)/shard_map/ppermute | solution.py:290
  111.3 22.3 %all-to-all-start.3 = ((f32[32,24,128]{2,1,0:T(8,128)}), f32[32,24,128]{2,1,0:T(8,128)S(1)}, u32[]{:S(2)}, u32[]{:S(2)}) async-start(f32[32,24,128]{2,1,0:T(8,128)} %broadcast_in_dim.41), calls=%async_computation.3 | async-start | bytes 786432 | tf_op jit(solution)/shard_map/all_to_all | solution.py:259

commit v4 on v2

--- a/solution.py
+++ b/solution.py
@@ -13,7 +13,8 @@
 TOP = math.sqrt(12.0)
 STEPS = 65535.0
 HALF = 32768.0
-GROUP = 16
+GROUP = 4
+LAG = 1
 
 
 def dft_tables(window):
@@ -23,13 +24,13 @@
     sine = np.sin(angles) / np.sqrt(window)
     first = np.block([[cosine, -sine], [sine, cosine]])
     second = np.block([[cosine, sine], [-sine, cosine]])
-    tables = []
+    down, across = [], []
     for table in (first, second):
         high = table.astype(np.float32).astype(BF16)
         low = (table - high.astype(np.float64)).astype(np.float32).astype(BF16)
-        tables.append(np.concatenate([high, low], axis=0))
-        tables.append(np.concatenate([high, low], axis=1))
-    return tables
+        down.append(np.concatenate([high, low], axis=0))
+        across.append(np.concatenate([high, low], axis=1))
+    return np.stack(down), np.stack(across)
 
 
 def split(value):
@@ -47,14 +48,15 @@
     return jnp.dot(table, jnp.concatenate([high, high], axis=0), preferred_element_type=F32)
 
 
-def pack_kernel(positions, measured, packed):
+def pack_kernel(positions, measured, low, packed):
+    del low
     patterns = measured.shape[0]
     slots, rows, window = packed.shape
     packed[...] = jnp.zeros(packed.shape, jnp.int16)
     lane = lax.broadcasted_iota(jnp.int32, (rows - window, window), 1)
     for p in range(patterns):
-        row = positions[p, 0]
-        column = positions[p, 1]
+        row = positions[0, p]
+        column = positions[1, p]
         tile = column // (3 * window)
         start = column - tile * (3 * window) - 2 * window
         amplitude = jnp.sqrt(measured[p]) * (STEPS / TOP)
@@ -65,7 +67,7 @@
 
 
 def main_kernel(
-    notes, received, own, margin, probe, first_down, first_across, second_down, second_across,
+    notes, received, own, margin, probe, down, across,
     sums, shifts, strip, total, probe_total, probe_full,
 ):
     slots = received.shape[0]
@@ -134,41 +136,48 @@
             total[part, 0, rows, :] += jnp.where(lane >= start, turned, 0.0)
             total[part, 1, rows, :] += jnp.where(lane < start, turned, 0.0)
 
-    def several(slots_now):
+    def stages(slots_now):
         cuts = [cut(slot) for slot in slots_now]
         exits = [e for w in cuts for e in leave(*w)]
-        field = both_ways(exits, first_down[...], second_across[...])
+        half = rows_first(exits, down[0])
+        yield
+        field = columns_next(half, across[1])
+        yield
         scaled = []
         for u, slot in enumerate(slots_now):
             mine = field[u * modes:(u + 1) * modes]
             scaling = scale_of(slot, mine)
             scaled += [jnp.concatenate([scaling * b[0], scaling * b[1]], axis=1) for b in mine]
-        back = both_ways(scaled, second_down[...], first_across[...])
+        half = rows_first(scaled, down[1])
+        yield
+        back = columns_next(half, across[0])
+        yield
         for u, slot in enumerate(slots_now):
             finish(slot, *cuts[u], back[u * modes:(u + 1) * modes])
 
-    def both_ways(blocks, down, across):
-        count = len(blocks)
+    def rows_first(blocks, down):
         half = from_right(jnp.concatenate(blocks, axis=0), down)
-        pieces = [
+        return [
             [half[b * window:(b + 1) * window, c * window:(c + 1) * window] for c in range(2)]
-            for b in range(count)
+            for b in range(len(blocks))
         ]
+
+    def columns_next(pieces, across):
         stacked = jnp.concatenate(
             [jnp.concatenate([p[c] for p in pieces], axis=1) for c in range(2)], axis=0
         )
         out = from_left(across, stacked)
         return [
             [out[c * window:(c + 1) * window, b * window:(b + 1) * window] for c in range(2)]
-            for b in range(count)
+            for b in range(len(pieces))
         ]
 
-    def step(at, carry):
-        several([GROUP * at + u for u in range(GROUP)])
-        return carry
-
     shifts[...] = jnp.zeros(shifts.shape, F32)
-    lax.fori_loop(0, slots // GROUP, step, 0)
+    flows = [stages(range(at, at + GROUP)) for at in range(0, slots, GROUP)]
+    for tick in range(5 + LAG * (len(flows) - 1)):
+        for at, flow in enumerate(flows):
+            if 0 <= tick - LAG * at < 5:
+                next(flow, None)
     deep = height // bands
     piece = 2 * modes * window // bands
     for b in range(bands):
@@ -187,7 +196,7 @@
         sums[b, 4 * deep:, :] = jnp.concatenate(parts, axis=0).astype(BF16)
 
 
-def pack(positions, measured, slots):
+def pack(positions, measured, low, slots):
     window = measured.shape[2]
     return pl.pallas_call(
         pack_kernel,
@@ -195,10 +204,11 @@
         in_specs=[
             pl.BlockSpec(memory_space=pltpu.SMEM),
             pl.BlockSpec(memory_space=pltpu.VMEM),
+            pl.BlockSpec(memory_space=pl.ANY),
         ],
         out_specs=pl.BlockSpec(memory_space=pltpu.VMEM),
         compiler_params=pltpu.CompilerParams(vmem_limit_bytes=16 * 2**20),
-    )(positions, measured)
+    )(positions.T, measured, low)
 
 
 def compute(notes, received, object_field, margin, probe, bands):
@@ -250,31 +260,29 @@
     patterns = measured.shape[0]
     deep = height // bands
     piece = 2 * modes * window // bands
-    margin = lax.ppermute(
-        object_field[:, :, :window].astype(BF16), "tile", [(t, t - 1) for t in range(1, tiles)]
-    )
-    received = exchange(pack(positions, measured, tiles), "tile")
+    low = object_field[:, :, :window].astype(BF16)
+    margin = lax.ppermute(low, "tile", [(t, t - 1) for t in range(1, tiles)])
+    received = exchange(pack(positions, measured, low, tiles), "tile")
     notes = received[:, window, :3].astype(jnp.int32)
     sums, shifts = compute(notes, received, object_field, margin, probe, bands)
     gathered = jnp.sum(exchange(sums, "scan").astype(F32), axis=0)
     strips = gathered[:4 * deep].reshape(2, 2, deep, window)
-    spilled = lax.ppermute(strips[:, 1], "tile", [(t, t + 1) for t in range(tiles - 1)])
-    object_grad = jnp.concatenate(
-        [spilled, jnp.zeros((2, deep, width - 2 * window), F32), strips[:, 0]], axis=2
-    )
     own_piece = gathered[4 * deep:4 * deep + piece]
     outgoing = jnp.concatenate(
         [jnp.broadcast_to(own_piece[None], (tiles, piece, window)), shifts], axis=1
     )
     mixed = exchange(outgoing, "tile")
     full_piece = jnp.sum(mixed[:, :piece], axis=0) / math.sqrt(patterns * bands * tiles)
-    probe_grad = exchange(
-        jnp.broadcast_to(full_piece[None], (bands, piece, window)), "scan"
-    ).reshape(modes, 2, window, window)
+    copies = jnp.broadcast_to(full_piece.astype(BF16)[None], (bands, piece, window))
+    probe_grad = exchange(copies, "scan").astype(F32).reshape(modes, 2, window, window)
     per_tile = jnp.sum(mixed[:, piece:piece + 2], axis=2) / window
     left_tile = positions[:, 1] // width
     hits = left_tile[:, None] == jnp.arange(tiles, dtype=jnp.int32)[None, :]
     position_grad = jnp.sum(jnp.where(hits[:, :, None], per_tile[None], 0.0), axis=1)
+    spilled = lax.ppermute(strips[:, 1], "tile", [(t, t + 1) for t in range(tiles - 1)])
+    object_grad = jnp.concatenate(
+        [spilled, jnp.zeros((2, deep, width - 2 * window), F32), strips[:, 0]], axis=2
+    )
     return (object_grad, probe_grad, position_grad)
 
 

time: 120 us -> 118 us (0.983)
  blocking collectives: 33.1 us -> 0 us
  waiting for transfers between devices: 37.7 us -> 56.9 us
  starting transfers between devices: 27.7 us -> 39.2 us
    all_to_all x1 -> x0, blocking collectives: 33.1 us -> none  [exchange(): return lax.all_to_all(value, axis, split_axis=0, concat_axis=0, tiled=True)]
    all_to_all x3 -> x4, waiting for transfers between devices: 37.7 us -> 56.1 us  [exchange(): return lax.all_to_all(value, axis, split_axis=0, concat_axis=0, tiled=True)]
    all_to_all x3 -> x4, starting transfers between devices: 22.1 us -> 33.5 us  [exchange(): return lax.all_to_all(value, axis, split_axis=0, concat_axis=0, tiled=True)]
    unnamed x19 -> x15, local copies, waits for them, and re-layouts: 3.69 us -> 2.74 us
  transfers between devices with their start and end apart: 5 -> 6, of which waited for: 3 -> 5; matrix products, arithmetic and copies ran while one was open for 3% -> 1% of each run, Pallas kernels for 0% -> 0%
where the time goes in v4:
time: 118 us
  waiting for transfers between devices  56.9 us (48%)
  starting transfers between devices  39.2 us (33%)
  Pallas kernels  12.9 us (11%)
  local copies, waits for them, and re-layouts  4.71 us (4%)
  other arithmetic  3.12 us (3%)
    all_to_all x4, waiting for transfers between devices, exchange(): return lax.all_to_all(value, axis, split_axis=0, concat_axis=0, tiled=True)  56.1 us
    all_to_all x4, starting transfers between devices, exchange(): return lax.all_to_all(value, axis, split_axis=0, concat_axis=0, tiled=True)  33.5 us
    pallas_call x1, Pallas kernels, compute(): pl.pallas_call(main_kernel, grid=(1,), out_shape=(jax.ShapeDtypeStruct((b...  11.2 us
    ppermute x1, starting transfers between devices, local(): lax.ppermute(strips[:, 1], 'tile', [(t, t + 1) for t in range(tiles - 1)])  3.54 us
    unnamed x15, local copies, waits for them, and re-layouts  2.74 us
  transfers between devices with their start and end apart: 6, of which 5 were waited for; matrix products, arithmetic and copies ran while one was open for 1% of the time, Pallas kernels for 0%

profile of v4, /device:TPU:1, one launch (start us, length us, event | category | flops | bytes accessed | tf_op | source)
XLA Modules:
  0.0 117.6 jit_solution(5338497715068354369)
XLA Ops:
  0.6 0.0 copy-start.1
  0.6 0.0 copy-start.2
  0.7 1.2 %slice.52.low = bf16[2,512,128]{2,1,0:T(8,128)(2,1)S(1)} slice(f32[2,512,384]{2,1,0:T(8,128)} %own.1), slice={[0:2], [0:512], [0:128]} | slice | bytes 524288 | tf_op jit(solution)/shard_map/slice | solution.py:263
  1.9 0.0 copy-start.3
  1.9 1.0 copy-done.3
  2.9 0.7 copy-done.5
  3.6 1.7 %shard_map.85 = s16[16,144,128]{2,1,0:T(8,128)(2,1)} custom-call(s32[2,8]{1,0:T(2,128)S(1)} %bitcast.14, f32[8,128,128]{2,1,0:T(8,128)S(1)} %copy-done.3, bf16[2,512,128]{2,1,0:T(8,128)(2,1)S(1)} %slice.52.low), custom_call_target="tpu_custom_call" | custom-call | tf_op jit(solution)/shard_map/pallas_call | solution.py:201
  5.3 10.2 %all-to-all-start = ((s16[16,144,128]{2,1,0:T(8,128)(2,1)}), s16[16,144,128]{2,1,0:T(8,128)(2,1)S(1)}, u32[]{:S(2)}, u32[]{:S(2)}) async-start(s16[16,144,128]{2,1,0:T(8,128)(2,1)} %shard_map.85), calls=%async_computation | async-start | bytes 1179648 | tf_op jit(solution)/shard_map/all_to_all | solution.py:251
  15.5 2.1 %collective-permute-start = (bf16[2,512,128]{2,1,0:T(8,128)(2,1)S(1)}, bf16[2,512,128]{2,1,0:T(8,128)(2,1)}, u32[]{:S(2)}, u32[]{:S(2)}) collective-permute-start(bf16[2,512,128]{2,1,0:T(8,128)(2,1)S(1)} %slice.52.low), channel_id=1, source_target_pairs={{1,0},{2,1},{3,2},{4,3},{5,4},{6,5},{7,6},{8,7},{9,8},{10,9},{11,1... | collective-permute-start | bytes 786440 | tf_op jit(solution)/shard_map/ppermute | solution.py:264
  17.7 16.5 %all-to-all-done.received = s16[16,144,128]{2,1,0:T(8,128)(2,1)S(1)} async-done(((s16[16,144,128]{2,1,0:T(8,128)(2,1)}), s16[16,144,128]{2,1,0:T(8,128)(2,1)S(1)}, u32[]{:S(2)}, u32[]{:S(2)}) %all-to-all-start) | async-done | bytes 589856 | tf_op jit(solution)/shard_map/all_to_all | solution.py:251
  34.2 0.0 collective-permute-done.margin
  34.2 0.0 copy-done.1
  34.2 0.0 copy-start.4
  34.3 0.9 copy-done.4
  35.2 11.2 %shard_map.86 = (bf16[32,96,128]{2,1,0:T(8,128)(2,1)}, f32[16,8,128]{2,1,0:T(8,128)S(1)}) custom-call(s32[16,3]{1,0:T(8,128)S(1)} %bitcast.13, s16[16,144,128]{2,1,0:T(8,128)(2,1)S(1)} %all-to-all-done.received, f32[2,512,384]{2,1,0:T(8,128)S(1)} %copy-done, bf16[2,512,128]{2,1,0:T(8,128)(2,1)} %collective-permute-done.margin, ...), custom_call_target="tpu_custom_call" | custom-call | tf_op jit(solution)/shard_map/pallas_call | solution.py:225
  46.4 11.4 %all-to-all-start.1 = ((bf16[32,96,128]{2,1,0:T(8,128)(2,1)}), bf16[32,96,128]{2,1,0:T(8,128)(2,1)S(1)}, u32[]{:S(2)}, u32[]{:S(2)}) async-start(bf16[32,96,128]{2,1,0:T(8,128)(2,1)} %get-tuple-element.5), calls=%async_computation.1 | async-start | bytes 1572864 | tf_op jit(solution)/shard_map/all_to_all | solution.py:251
  57.9 21.8 %all-to-all-done.1 = bf16[32,96,128]{2,1,0:T(8,128)(2,1)S(1)} async-done(((bf16[32,96,128]{2,1,0:T(8,128)(2,1)}), bf16[32,96,128]{2,1,0:T(8,128)(2,1)S(1)}, u32[]{:S(2)}, u32[]{:S(2)}) %all-to-all-start.1) | async-done | bytes 786464 | tf_op jit(solution)/shard_map/all_to_all | solution.py:251
  79.7 0.1 convert_reduce_fusion
  79.8 0.7 pad_maximum_fusion
  80.6 6.6 %all-to-all-start.2 = ((f32[16,32,128]{2,1,0:T(8,128)}), f32[16,32,128]{2,1,0:T(8,128)S(1)}, u32[]{:S(2)}, u32[]{:S(2)}) async-start(f32[16,32,128]{2,1,0:T(8,128)} %pad_maximum_fusion), calls=%async_computation.2 | async-start | bytes 524288 | tf_op jit(solution)/shard_map/all_to_all | solution.py:251
  87.2 3.5 %collective-permute-start.1 = (f32[2,16,128]{2,1,0:T(8,128)S(1)}, f32[2,16,128]{2,1,0:T(8,128)S(1)}, u32[]{:S(2)}, u32[]{:S(2)}) collective-permute-start(f32[2,16,128]{2,1,0:T(8,128)S(1)} %get-tuple-element.7), channel_id=1, source_target_pairs={{0,1},{1,2},{2,3},{3,4},{4,5},{5,6},{6,7},{7,8},{8,9},{9,10},{10,1... | collective-permute-start | bytes 49160 | tf_op jit(solution)/shard_map/ppermute | solution.py:282
  90.8 0.1 iota_compare_fusion
  90.9 0.8 collective-permute-done.1
  91.6 0.6 pad_maximum_fusion.1
  92.2 6.9 %all-to-all-done.2 = f32[16,32,128]{2,1,0:T(8,128)S(1)} async-done(((f32[16,32,128]{2,1,0:T(8,128)}), f32[16,32,128]{2,1,0:T(8,128)S(1)}, u32[]{:S(2)}, u32[]{:S(2)}) %all-to-all-start.2) | async-done | bytes 262176 | tf_op jit(solution)/shard_map/all_to_all | solution.py:251
  99.2 0.7 broadcast_in_dim.41
  99.9 5.2 %all-to-all-start.3 = ((bf16[32,24,128]{2,1,0:T(8,128)(2,1)}), bf16[32,24,128]{2,1,0:T(8,128)(2,1)S(1)}, u32[]{:S(2)}, u32[]{:S(2)}) async-start(bf16[32,24,128]{2,1,0:T(8,128)(2,1)} %broadcast_in_dim.41), calls=%async_computation.3 | async-start | bytes 393216 | tf_op jit(solution)/shard_map/all_to_all | solution.py:251
  105.1 0.1 slice_reduce_fusion.1
  105.2 0.1 copy.28
  105.3 0.7 select_reduce_fusion
  106.0 10.9 %all-to-all-done.3 = bf16[32,24,128]{2,1,0:T(8,128)(2,1)S(1)} async-done(((bf16[32,24,128]{2,1,0:T(8,128)(2,1)}), bf16[32,24,128]{2,1,0:T(8,128)(2,1)S(1)}, u32[]{:S(2)}, u32[]{:S(2)}) %all-to-all-start.3) | async-done | bytes 196640 | tf_op jit(solution)/shard_map/all_to_all | solution.py:251
  116.9 0.8 convert.6
  (17 shorter events, 0.1 us)
Async XLA Ops:
  0.6 33.6 %copy-start.1 = (bf16[2,512,256]{2,1,0:T(8,128)(2,1)S(1)}, bf16[2,512,256]{2,1,0:T(8,128)(2,1)}, u32[]{:S(2)}) copy-start(bf16[2,512,256]{2,1,0:T(8,128)(2,1)} %constant.24.clone.down) | copy-start | bytes 1572868
  0.6 33.6 %copy-start.2 = (bf16[2,256,512]{2,1,0:T(8,128)(2,1)S(1)}, bf16[2,256,512]{2,1,0:T(8,128)(2,1)}, u32[]{:S(2)}) copy-start(bf16[2,256,512]{2,1,0:T(8,128)(2,1)} %constant.25.clone.across) | copy-start | bytes 1572868
  0.7 33.6 %copy-start = (f32[2,512,384]{2,1,0:T(8,128)S(1)}, f32[2,512,384]{2,1,0:T(8,128)}, u32[]{:S(2)}) copy-start(f32[2,512,384]{2,1,0:T(8,128)} %own.1) | copy-start | bytes 4718596
  1.9 1.0 copy-start.3
  2.9 0.7 copy-start.5
  5.3 28.9 %all-to-all-start = ((s16[16,144,128]{2,1,0:T(8,128)(2,1)}), s16[16,144,128]{2,1,0:T(8,128)(2,1)S(1)}, u32[]{:S(2)}, u32[]{:S(2)}) async-start(s16[16,144,128]{2,1,0:T(8,128)(2,1)} %shard_map.85), calls=%async_computation | async-start | bytes 1179648 | tf_op jit(solution)/shard_map/all_to_all | solution.py:251
  15.5 18.7 %collective-permute-start = (bf16[2,512,128]{2,1,0:T(8,128)(2,1)S(1)}, bf16[2,512,128]{2,1,0:T(8,128)(2,1)}, u32[]{:S(2)}, u32[]{:S(2)}) collective-permute-start(bf16[2,512,128]{2,1,0:T(8,128)(2,1)S(1)} %slice.52.low), channel_id=1, source_target_pairs={{1,0},{2,1},{3,2},{4,3},{5,4},{6,5},{7,6},{8,7},{9,8},{10,9},{11,1... | collective-permute-start | bytes 786440 | tf_op jit(solution)/shard_map/ppermute | solution.py:264
  34.2 0.9 copy-start.4
  46.4 11.4 %copy-start.6 = (s32[8,2]{0,1:T(2,128)S(1)}, s32[8,2]{0,1:T(2,128)}, u32[]{:S(2)}) copy-start(s32[8,2]{0,1:T(2,128)} %param.9) | copy-start | bytes 196
  46.4 33.3 %all-to-all-start.1 = ((bf16[32,96,128]{2,1,0:T(8,128)(2,1)}), bf16[32,96,128]{2,1,0:T(8,128)(2,1)S(1)}, u32[]{:S(2)}, u32[]{:S(2)}) async-start(bf16[32,96,128]{2,1,0:T(8,128)(2,1)} %get-tuple-element.5), calls=%async_computation.1 | async-start | bytes 1572864 | tf_op jit(solution)/shard_map/all_to_all | solution.py:251
  80.6 18.6 %all-to-all-start.2 = ((f32[16,32,128]{2,1,0:T(8,128)}), f32[16,32,128]{2,1,0:T(8,128)S(1)}, u32[]{:S(2)}, u32[]{:S(2)}) async-start(f32[16,32,128]{2,1,0:T(8,128)} %pad_maximum_fusion), calls=%async_computation.2 | async-start | bytes 524288 | tf_op jit(solution)/shard_map/all_to_all | solution.py:251
  87.2 4.4 %collective-permute-start.1 = (f32[2,16,128]{2,1,0:T(8,128)S(1)}, f32[2,16,128]{2,1,0:T(8,128)S(1)}, u32[]{:S(2)}, u32[]{:S(2)}) collective-permute-start(f32[2,16,128]{2,1,0:T(8,128)S(1)} %get-tuple-element.7), channel_id=1, source_target_pairs={{0,1},{1,2},{2,3},{3,4},{4,5},{5,6},{6,7},{7,8},{8,9},{9,10},{10,1... | collective-permute-start | bytes 49160 | tf_op jit(solution)/shard_map/ppermute | solution.py:282
  99.9 17.0 %all-to-all-start.3 = ((bf16[32,24,128]{2,1,0:T(8,128)(2,1)}), bf16[32,24,128]{2,1,0:T(8,128)(2,1)S(1)}, u32[]{:S(2)}, u32[]{:S(2)}) async-start(bf16[32,24,128]{2,1,0:T(8,128)(2,1)} %broadcast_in_dim.41), calls=%async_computation.3 | async-start | bytes 393216 | tf_op jit(solution)/shard_map/all_to_all | solution.py:251

commit v5 on v4

--- a/solution.py
+++ b/solution.py
@@ -48,40 +48,51 @@
     return jnp.dot(table, jnp.concatenate([high, high], axis=0), preferred_element_type=F32)
 
 
-def pack_kernel(positions, measured, low, packed):
-    del low
+def pack_kernel(positions, measured, packed, places, loaded, place_sem, load_sems):
     patterns = measured.shape[0]
     slots, rows, window = packed.shape
+    place = pltpu.make_async_copy(positions, places, place_sem)
+    place.start()
+    loads = [
+        pltpu.make_async_copy(measured.at[p], loaded.at[p], load_sems.at[p]) for p in range(patterns)
+    ]
+    for load in loads:
+        load.start()
     packed[...] = jnp.zeros(packed.shape, jnp.int16)
     lane = lax.broadcasted_iota(jnp.int32, (rows - window, window), 1)
+    place.wait()
     for p in range(patterns):
-        row = positions[0, p]
-        column = positions[1, p]
+        row = places[0, p]
+        column = places[1, p]
         tile = column // (3 * window)
         start = column - tile * (3 * window) - 2 * window
-        amplitude = jnp.sqrt(measured[p]) * (STEPS / TOP)
+        note = jnp.where(lane == 0, row, jnp.where(lane == 1, start, jnp.where(lane == 2, 1, 0)))
+        packed[tile, window:rows, :] = note.astype(jnp.int16)
+        loads[p].wait()
+        amplitude = jnp.sqrt(loaded[p]) * (STEPS / TOP)
         level = jnp.clip(jnp.round(amplitude) - HALF, -HALF, HALF - 1.0)
         packed[tile, 0:window, :] = level.astype(jnp.int32).astype(jnp.int16)
-        note = jnp.where(lane == 0, row, jnp.where(lane == 1, start, jnp.where(lane == 2, 1, 0)))
-        packed[tile, window:rows, :] = note.astype(jnp.int16)
 
 
 def main_kernel(
     notes, received, own, margin, probe, down, across,
-    sums, shifts, strip, total, probe_total, probe_full,
+    probe_sums, sums, shifts, strip, total, probe_total, probe_full,
+    probe_near, probe_sem,
 ):
     slots = received.shape[0]
     modes = probe.shape[0]
     window = probe.shape[2]
     bands = sums.shape[0]
     height = own.shape[1]
+    fetch = pltpu.make_async_copy(probe, probe_near, probe_sem)
+    fetch.start()
     for part in range(2):
         strip[part, 0] = own[part].astype(BF16).astype(F32)
         strip[part, 1] = margin[part].astype(F32)
-        for m in range(modes):
-            probe_full[m, part] = probe[m, part].astype(F32)
     total[...] = jnp.zeros(total.shape, F32)
     probe_total[...] = jnp.zeros(probe_total.shape, F32)
+    fetch.wait()
+    probe_full[...] = probe_near[...].astype(F32)
     lane = lax.broadcasted_iota(jnp.int32, (window, window), 1)
     row = lax.broadcasted_iota(jnp.int32, (window, window), 0)
 
@@ -178,37 +189,38 @@
         for at, flow in enumerate(flows):
             if 0 <= tick - LAG * at < 5:
                 next(flow, None)
-    deep = height // bands
-    piece = 2 * modes * window // bands
     for b in range(bands):
+        deep = height // bands
         for part in range(2):
             for side in range(2):
                 at = (2 * part + side) * deep
                 sums[b, at:at + deep, :] = total[part, side, b * deep:(b + 1) * deep, :].astype(BF16)
-        mode, offset = divmod(b * piece, window)
-        parts = []
-        left = piece
+    piece = 2 * modes * window // slots
+    for t in range(slots):
+        mode, offset = divmod(t * piece, window)
+        left, at = piece, 0
         while left:
             take = min(left, window - offset)
-            parts.append(probe_total[mode, offset:offset + take, :])
-            mode, offset, left = mode + 1, 0, left - take
-        parts.append(jnp.zeros((sums.shape[1] - 4 * deep - piece, window), F32))
-        sums[b, 4 * deep:, :] = jnp.concatenate(parts, axis=0).astype(BF16)
-
-
-def pack(positions, measured, low, slots):
-    window = measured.shape[2]
+            probe_sums[t, at:at + take, :] = probe_total[mode, offset:offset + take, :].astype(BF16)
+            mode, offset, left, at = mode + 1, 0, left - take, at + take
+        probe_sums[t, piece:, :] = jnp.concatenate(split(shifts[t]), axis=0)
+
+
+def pack(positions, measured, slots):
+    patterns, window = measured.shape[0], measured.shape[2]
     return pl.pallas_call(
         pack_kernel,
         out_shape=jax.ShapeDtypeStruct((slots, window + 16, window), jnp.int16),
-        in_specs=[
-            pl.BlockSpec(memory_space=pltpu.SMEM),
-            pl.BlockSpec(memory_space=pltpu.VMEM),
-            pl.BlockSpec(memory_space=pl.ANY),
+        in_specs=[pl.BlockSpec(memory_space=pltpu.HBM)] * 2,
+        out_specs=pl.BlockSpec(memory_space=pltpu.VMEM),
+        scratch_shapes=[
+            pltpu.SMEM((2, patterns), jnp.int32),
+            pltpu.VMEM(measured.shape, F32),
+            pltpu.SemaphoreType.DMA,
+            pltpu.SemaphoreType.DMA((patterns,)),
         ],
-        out_specs=pl.BlockSpec(memory_space=pltpu.VMEM),
-        compiler_params=pltpu.CompilerParams(vmem_limit_bytes=16 * 2**20),
-    )(positions.T, measured, low)
+        compiler_params=pltpu.CompilerParams(vmem_limit_bytes=60 * 2**20),
+    )(positions.T, measured)
 
 
 def compute(notes, received, object_field, margin, probe, bands):
@@ -221,27 +233,31 @@
     def whole(shape):
         return pl.BlockSpec(shape, lambda i: (0,) * len(shape))
 
-    rows = 4 * (height // bands) + -(-(2 * modes * window // bands) // 16) * 16
+    probe_shape = (slots, 2 * modes * window // slots + 16, window)
+    sums_shape = (bands, 4 * (height // bands), window)
     return pl.pallas_call(
         main_kernel,
         grid=(1,),
         out_shape=(
-            jax.ShapeDtypeStruct((bands, rows, window), BF16),
-            jax.ShapeDtypeStruct((slots, 8, window), F32),
+            jax.ShapeDtypeStruct(probe_shape, BF16),
+            jax.ShapeDtypeStruct(sums_shape, BF16),
         ),
         in_specs=[
             pl.BlockSpec(memory_space=pltpu.SMEM),
             whole(received.shape),
             pl.BlockSpec((2, height, window), lambda i: (0, 0, 2)),
             whole(margin.shape),
-            whole(probe.shape),
+            pl.BlockSpec(memory_space=pltpu.HBM),
         ] + [whole(table.shape) for table in tables],
-        out_specs=(whole((bands, rows, window)), whole((slots, 8, window))),
+        out_specs=(whole(probe_shape), whole(sums_shape)),
         scratch_shapes=[
+            pltpu.VMEM((slots, 8, window), F32),
             pltpu.VMEM((2, 2, height, window), F32),
             pltpu.VMEM((2, 2, height, window), F32),
             pltpu.VMEM((2 * modes, window, window), F32),
             pltpu.VMEM((modes, 2, window, window), F32),
+            pltpu.VMEM((modes, 2, window, window), BF16),
+            pltpu.SemaphoreType.DMA,
         ],
         compiler_params=pltpu.CompilerParams(vmem_limit_bytes=40 * 2**20),
     )(notes, received, object_field, margin, probe, *tables)
@@ -259,30 +275,33 @@
     modes, window = probe.shape[0], probe.shape[2]
     patterns = measured.shape[0]
     deep = height // bands
-    piece = 2 * modes * window // bands
-    low = object_field[:, :, :window].astype(BF16)
-    margin = lax.ppermute(low, "tile", [(t, t - 1) for t in range(1, tiles)])
-    received = exchange(pack(positions, measured, low, tiles), "tile")
+    piece = 2 * modes * window // tiles
+    margin = lax.ppermute(
+        object_field[:, :, :window].astype(BF16), "tile", [(t, t - 1) for t in range(1, tiles)]
+    )
+    received = exchange(pack(positions, measured, tiles), "tile")
     notes = received[:, window, :3].astype(jnp.int32)
-    sums, shifts = compute(notes, received, object_field, margin, probe, bands)
-    gathered = jnp.sum(exchange(sums, "scan").astype(F32), axis=0)
+    probe_sums, sums = compute(notes, received, object_field, margin, probe, bands)
+    mixed = exchange(probe_sums, "tile").astype(F32)
+    tile_piece = jnp.sum(mixed[:, :piece], axis=0).astype(BF16)
+    everything = exchange(
+        jnp.concatenate([sums, jnp.broadcast_to(tile_piece[None], (bands, piece, window))], axis=1),
+        "scan",
+    )
+    gathered = jnp.sum(everything.astype(F32), axis=0)
+    full_piece = gathered[4 * deep:] / math.sqrt(patterns * bands * tiles)
+    probe_grad = exchange(
+        jnp.broadcast_to(full_piece.astype(BF16)[None], (tiles, piece, window)), "tile"
+    ).astype(F32).reshape(modes, 2, window, window)
     strips = gathered[:4 * deep].reshape(2, 2, deep, window)
-    own_piece = gathered[4 * deep:4 * deep + piece]
-    outgoing = jnp.concatenate(
-        [jnp.broadcast_to(own_piece[None], (tiles, piece, window)), shifts], axis=1
-    )
-    mixed = exchange(outgoing, "tile")
-    full_piece = jnp.sum(mixed[:, :piece], axis=0) / math.sqrt(patterns * bands * tiles)
-    copies = jnp.broadcast_to(full_piece.astype(BF16)[None], (bands, piece, window))
-    probe_grad = exchange(copies, "scan").astype(F32).reshape(modes, 2, window, window)
-    per_tile = jnp.sum(mixed[:, piece:piece + 2], axis=2) / window
-    left_tile = positions[:, 1] // width
-    hits = left_tile[:, None] == jnp.arange(tiles, dtype=jnp.int32)[None, :]
-    position_grad = jnp.sum(jnp.where(hits[:, :, None], per_tile[None], 0.0), axis=1)
     spilled = lax.ppermute(strips[:, 1], "tile", [(t, t + 1) for t in range(tiles - 1)])
     object_grad = jnp.concatenate(
         [spilled, jnp.zeros((2, deep, width - 2 * window), F32), strips[:, 0]], axis=2
     )
+    per_tile = jnp.sum(mixed[:, piece:piece + 2] + mixed[:, piece + 8:piece + 10], axis=2) / window
+    left_tile = positions[:, 1] // width
+    hits = left_tile[:, None] == jnp.arange(tiles, dtype=jnp.int32)[None, :]
+    position_grad = jnp.sum(jnp.where(hits[:, :, None], per_tile[None], 0.0), axis=1)
     return (object_grad, probe_grad, position_grad)
 
 

time: 118 us -> 114 us (0.966)
  blocking collectives: 0 us -> 16.8 us
  waiting for transfers between devices: 56.9 us -> 46 us
  starting transfers between devices: 39.2 us -> 32 us
  local copies, waits for them, and re-layouts: 4.71 us -> 2.54 us
    all_to_all x0 -> x1, blocking collectives: none -> 16.8 us  [exchange(): return lax.all_to_all(value, axis, split_axis=0, concat_axis=0, tiled=True)]
    all_to_all x4 -> x3, waiting for transfers between devices: 56.1 us -> 45.8 us  [exchange(): return lax.all_to_all(value, axis, split_axis=0, concat_axis=0, tiled=True)]
    all_to_all x4 -> x3, starting transfers between devices: 33.5 us -> 26.3 us  [exchange(): return lax.all_to_all(value, axis, split_axis=0, concat_axis=0, tiled=True)]
    unnamed x15 -> x10, local copies, waits for them, and re-layouts: 2.74 us -> 0.95 us
  transfers between devices with their start and end apart: 6 -> 5, of which waited for: 5 -> 4; matrix products, arithmetic and copies ran while one was open for 1% -> 2% of each run, Pallas kernels for 0% -> 0%
where the time goes in v5:
time: 114 us
  waiting for transfers between devices  46 us (40%)
  starting transfers between devices  32 us (28%)
  blocking collectives  16.8 us (15%)
  Pallas kernels  12.4 us (11%)
  other arithmetic  3.44 us (3%)
  local copies, waits for them, and re-layouts  2.54 us (2%)
    all_to_all x3, waiting for transfers between devices, exchange(): return lax.all_to_all(value, axis, split_axis=0, concat_axis=0, tiled=True)  45.8 us
    all_to_all x3, starting transfers between devices, exchange(): return lax.all_to_all(value, axis, split_axis=0, concat_axis=0, tiled=True)  26.3 us
    all_to_all x1, blocking collectives, exchange(): return lax.all_to_all(value, axis, split_axis=0, concat_axis=0, tiled=True)  16.8 us
    pallas_call x1, Pallas kernels, compute(): pl.pallas_call(main_kernel, grid=(1,), out_shape=(jax.ShapeDtypeStruct(pr...  10.2 us
    ppermute x1, starting transfers between devices, local(): lax.ppermute(strips[:, 1], 'tile', [(t, t + 1) for t in range(tiles - 1)])  3.55 us
  transfers between devices with their start and end apart: 5, of which 4 were waited for; matrix products, arithmetic and copies ran while one was open for 2% of the time, Pallas kernels for 0%

profile of v5, /device:TPU:1, one launch (start us, length us, event | category | flops | bytes accessed | tf_op | source)
XLA Modules:
  0.0 114.0 jit_solution(15924920007605865275)
XLA Ops:
  0.6 0.0 copy-start.1
  0.6 0.0 copy-start
  0.7 0.0 copy-start.2
  0.7 2.2 %shard_map.85 = s16[16,144,128]{2,1,0:T(8,128)(2,1)} custom-call(s32[2,8]{1,0:T(2,128)} %bitcast.16, f32[8,128,128]{2,1,0:T(8,128)} %measured.1), custom_call_target="tpu_custom_call" | custom-call | tf_op jit(solution)/shard_map/pallas_call | solution.py:211
  2.9 10.3 %all-to-all-start = ((s16[16,144,128]{2,1,0:T(8,128)(2,1)}), s16[16,144,128]{2,1,0:T(8,128)(2,1)S(1)}, u32[]{:S(2)}, u32[]{:S(2)}) async-start(s16[16,144,128]{2,1,0:T(8,128)(2,1)} %shard_map.85), calls=%async_computation | async-start | bytes 1179648 | tf_op jit(solution)/shard_map/all_to_all | solution.py:267
  13.2 0.0 copy-done
  13.2 0.7 slice.63
  13.9 2.1 %collective-permute-start = (bf16[2,512,128]{2,1,0:T(8,128)(2,1)}, bf16[2,512,128]{2,1,0:T(8,128)(2,1)S(1)}, u32[]{:S(2)}, u32[]{:S(2)}) collective-permute-start(bf16[2,512,128]{2,1,0:T(8,128)(2,1)} %slice.63), channel_id=1, source_target_pairs={{1,0},{2,1},{3,2},{4,3},{5,4},{6,5},{7,6},{8,7},{9,8},{10,9},{11,1... | collective-permute-start | bytes 786440 | tf_op jit(solution)/shard_map/ppermute | solution.py:279
  16.0 15.8 %all-to-all-done.received = s16[16,144,128]{2,1,0:T(8,128)(2,1)S(1)} async-done(((s16[16,144,128]{2,1,0:T(8,128)(2,1)}), s16[16,144,128]{2,1,0:T(8,128)(2,1)S(1)}, u32[]{:S(2)}, u32[]{:S(2)}) %all-to-all-start) | async-done | bytes 589856 | tf_op jit(solution)/shard_map/all_to_all | solution.py:267
  31.8 0.0 collective-permute-done.margin
  31.8 0.0 copy-done.1
  31.9 0.0 copy-start.3
  31.9 0.9 copy-done.3
  32.8 10.2 %shard_map.86 = (bf16[16,64,128]{2,1,0:T(8,128)(2,1)S(1)}, bf16[32,64,128]{2,1,0:T(8,128)(2,1)S(1)}) custom-call(s32[16,3]{1,0:T(8,128)S(1)} %bitcast.13, s16[16,144,128]{2,1,0:T(8,128)(2,1)S(1)} %all-to-all-done.received, f32[2,512,384]{2,1,0:T(8,128)S(1)} %copy-done, bf16[2,512,128]{2,1,0:T(8,128)(2,1)S(1)} %collective-permute-done.margin, ...), custom_call_target="tpu_custom_call" | custom-call | tf_op jit(solution)/shard_map/pallas_call | solution.py:238
  43.0 16.8 %all_to_all.20 = bf16[16,64,128]{2,1,0:T(8,128)(2,1)S(1)} all-to-all(bf16[16,64,128]{2,1,0:T(8,128)(2,1)S(1)} %get-tuple-element.6), channel_id=1, replica_groups=mesh['scan'=32,'tile'=16] {'tile'}, dimensions={0} | all-to-all | bytes 524288 | tf_op jit(solution)/shard_map/all_to_all | solution.py:267
  59.8 0.1 broadcast_in_dim.19
  59.9 0.0 copy-start.4
  59.9 1.0 pad_maximum_fusion
  60.9 11.2 %all-to-all-start.2 = ((bf16[32,112,128]{2,1,0:T(8,128)(2,1)}), bf16[32,112,128]{2,1,0:T(8,128)(2,1)S(1)}, u32[]{:S(2)}, u32[]{:S(2)}) async-start(bf16[32,112,128]{2,1,0:T(8,128)(2,1)} %pad_maximum_fusion), calls=%async_computation.2 | async-start | bytes 1835008 | tf_op jit(solution)/shard_map/all_to_all | solution.py:267
  72.1 0.1 iota_compare_fusion
  72.2 0.1 fusion.1
  72.3 0.1 copy.24
  72.4 24.3 %all-to-all-done.2 = bf16[32,112,128]{2,1,0:T(8,128)(2,1)S(1)} async-done(((bf16[32,112,128]{2,1,0:T(8,128)(2,1)}), bf16[32,112,128]{2,1,0:T(8,128)(2,1)S(1)}, u32[]{:S(2)}, u32[]{:S(2)}) %all-to-all-start.2) | async-done | bytes 917536 | tf_op jit(solution)/shard_map/all_to_all | solution.py:267
  96.8 0.1 convert_reduce_fusion
  96.9 0.7 broadcast_in_dim.41
  97.6 4.9 %all-to-all-start.3 = ((bf16[16,48,128]{2,1,0:T(8,128)(2,1)}), bf16[16,48,128]{2,1,0:T(8,128)(2,1)S(1)}, u32[]{:S(2)}, u32[]{:S(2)}) async-start(bf16[16,48,128]{2,1,0:T(8,128)(2,1)} %broadcast_in_dim.41), calls=%async_computation.3 | async-start | bytes 393216 | tf_op jit(solution)/shard_map/all_to_all | solution.py:267
  102.5 3.5 %collective-permute-start.1 = (f32[2,16,128]{2,1,0:T(8,128)S(1)}, f32[2,16,128]{2,1,0:T(8,128)S(1)}, u32[]{:S(2)}, u32[]{:S(2)}) collective-permute-start(f32[2,16,128]{2,1,0:T(8,128)S(1)} %get-tuple-element.7), channel_id=1, source_target_pairs={{0,1},{1,2},{2,3},{3,4},{4,5},{5,6},{6,7},{7,8},{8,9},{9,10},{10,1... | collective-permute-start | bytes 49160 | tf_op jit(solution)/shard_map/ppermute | solution.py:297
  106.0 0.7 select_reduce_fusion
  106.7 0.2 collective-permute-done.1
  106.9 0.6 pad_maximum_fusion.1
  107.5 5.7 %all-to-all-done.3 = bf16[16,48,128]{2,1,0:T(8,128)(2,1)S(1)} async-done(((bf16[16,48,128]{2,1,0:T(8,128)(2,1)}), bf16[16,48,128]{2,1,0:T(8,128)(2,1)S(1)}, u32[]{:S(2)}, u32[]{:S(2)}) %all-to-all-start.3) | async-done | bytes 196640 | tf_op jit(solution)/shard_map/all_to_all | solution.py:267
  113.2 0.8 convert.6
  (12 shorter events, 0.1 us)
Async XLA Ops:
  0.6 31.2 %copy-start.1 = (bf16[2,256,512]{2,1,0:T(8,128)(2,1)S(1)}, bf16[2,256,512]{2,1,0:T(8,128)(2,1)}, u32[]{:S(2)}) copy-start(bf16[2,256,512]{2,1,0:T(8,128)(2,1)} %constant.25.clone.across) | copy-start | bytes 1572868
  0.6 12.5 %copy-start = (f32[2,512,384]{2,1,0:T(8,128)S(1)}, f32[2,512,384]{2,1,0:T(8,128)}, u32[]{:S(2)}) copy-start(f32[2,512,384]{2,1,0:T(8,128)} %own.1) | copy-start | bytes 4718596
  0.7 31.2 %copy-start.2 = (bf16[2,512,256]{2,1,0:T(8,128)(2,1)S(1)}, bf16[2,512,256]{2,1,0:T(8,128)(2,1)}, u32[]{:S(2)}) copy-start(bf16[2,512,256]{2,1,0:T(8,128)(2,1)} %constant.24.clone.down) | copy-start | bytes 1572868
  2.9 28.9 %all-to-all-start = ((s16[16,144,128]{2,1,0:T(8,128)(2,1)}), s16[16,144,128]{2,1,0:T(8,128)(2,1)S(1)}, u32[]{:S(2)}, u32[]{:S(2)}) async-start(s16[16,144,128]{2,1,0:T(8,128)(2,1)} %shard_map.85), calls=%async_computation | async-start | bytes 1179648 | tf_op jit(solution)/shard_map/all_to_all | solution.py:267
  13.9 17.9 %collective-permute-start = (bf16[2,512,128]{2,1,0:T(8,128)(2,1)}, bf16[2,512,128]{2,1,0:T(8,128)(2,1)S(1)}, u32[]{:S(2)}, u32[]{:S(2)}) collective-permute-start(bf16[2,512,128]{2,1,0:T(8,128)(2,1)} %slice.63), channel_id=1, source_target_pairs={{1,0},{2,1},{3,2},{4,3},{5,4},{6,5},{7,6},{8,7},{9,8},{10,9},{11,1... | collective-permute-start | bytes 786440 | tf_op jit(solution)/shard_map/ppermute | solution.py:279
  31.9 0.9 copy-start.3
  59.9 12.2 %copy-start.4 = (s32[8,2]{0,1:T(2,128)S(1)}, s32[8,2]{0,1:T(2,128)}, u32[]{:S(2)}) copy-start(s32[8,2]{0,1:T(2,128)} %param.9) | copy-start | bytes 196
  60.9 35.9 %all-to-all-start.2 = ((bf16[32,112,128]{2,1,0:T(8,128)(2,1)}), bf16[32,112,128]{2,1,0:T(8,128)(2,1)S(1)}, u32[]{:S(2)}, u32[]{:S(2)}) async-start(bf16[32,112,128]{2,1,0:T(8,128)(2,1)} %pad_maximum_fusion), calls=%async_computation.2 | async-start | bytes 1835008 | tf_op jit(solution)/shard_map/all_to_all | solution.py:267
  97.6 15.6 %all-to-all-start.3 = ((bf16[16,48,128]{2,1,0:T(8,128)(2,1)}), bf16[16,48,128]{2,1,0:T(8,128)(2,1)S(1)}, u32[]{:S(2)}, u32[]{:S(2)}) async-start(bf16[16,48,128]{2,1,0:T(8,128)(2,1)} %broadcast_in_dim.41), calls=%async_computation.3 | async-start | bytes 393216 | tf_op jit(solution)/shard_map/all_to_all | solution.py:267
  102.5 4.4 %collective-permute-start.1 = (f32[2,16,128]{2,1,0:T(8,128)S(1)}, f32[2,16,128]{2,1,0:T(8,128)S(1)}, u32[]{:S(2)}, u32[]{:S(2)}) collective-permute-start(f32[2,16,128]{2,1,0:T(8,128)S(1)} %get-tuple-element.7), channel_id=1, source_target_pairs={{0,1},{1,2},{2,3},{3,4},{4,5},{5,6},{6,7},{7,8},{8,9},{9,10},{10,1... | collective-permute-start | bytes 49160 | tf_op jit(solution)/shard_map/ppermute | solution.py:297

commit v6 on v5

--- a/solution.py
+++ b/solution.py
@@ -24,13 +24,12 @@
     sine = np.sin(angles) / np.sqrt(window)
     first = np.block([[cosine, -sine], [sine, cosine]])
     second = np.block([[cosine, sine], [-sine, cosine]])
-    down, across = [], []
+    tables = []
     for table in (first, second):
         high = table.astype(np.float32).astype(BF16)
         low = (table - high.astype(np.float64)).astype(np.float32).astype(BF16)
-        down.append(np.concatenate([high, low], axis=0))
-        across.append(np.concatenate([high, low], axis=1))
-    return np.stack(down), np.stack(across)
+        tables += [high, low]
+    return [np.stack(tables)]
 
 
 def split(value):
@@ -75,7 +74,7 @@
 
 
 def main_kernel(
-    notes, received, own, margin, probe, down, across,
+    notes, received, own, margin, probe, tables,
     probe_sums, sums, shifts, strip, total, probe_total, probe_full,
     probe_near, probe_sem,
 ):
@@ -147,21 +146,24 @@
             total[part, 0, rows, :] += jnp.where(lane >= start, turned, 0.0)
             total[part, 1, rows, :] += jnp.where(lane < start, turned, 0.0)
 
+    def joined(at, axis):
+        return jnp.concatenate([tables[2 * at], tables[2 * at + 1]], axis=axis)
+
     def stages(slots_now):
         cuts = [cut(slot) for slot in slots_now]
         exits = [e for w in cuts for e in leave(*w)]
-        half = rows_first(exits, down[0])
+        half = rows_first(exits, joined(0, 0))
         yield
-        field = columns_next(half, across[1])
+        field = columns_next(half, joined(1, 1))
         yield
         scaled = []
         for u, slot in enumerate(slots_now):
             mine = field[u * modes:(u + 1) * modes]
             scaling = scale_of(slot, mine)
             scaled += [jnp.concatenate([scaling * b[0], scaling * b[1]], axis=1) for b in mine]
-        half = rows_first(scaled, down[1])
+        half = rows_first(scaled, joined(1, 0))
         yield
-        back = columns_next(half, across[0])
+        back = columns_next(half, joined(0, 1))
         yield
         for u, slot in enumerate(slots_now):
             finish(slot, *cuts[u], back[u * modes:(u + 1) * modes])
@@ -234,7 +236,7 @@
         return pl.BlockSpec(shape, lambda i: (0,) * len(shape))
 
     probe_shape = (slots, 2 * modes * window // slots + 16, window)
-    sums_shape = (bands, 4 * (height // bands), window)
+    sums_shape = (bands, 4 * (height // bands) + 2 * modes * window // slots, window)
     return pl.pallas_call(
         main_kernel,
         grid=(1,),
@@ -284,10 +286,8 @@
     probe_sums, sums = compute(notes, received, object_field, margin, probe, bands)
     mixed = exchange(probe_sums, "tile").astype(F32)
     tile_piece = jnp.sum(mixed[:, :piece], axis=0).astype(BF16)
-    everything = exchange(
-        jnp.concatenate([sums, jnp.broadcast_to(tile_piece[None], (bands, piece, window))], axis=1),
-        "scan",
-    )
+    copies = jnp.broadcast_to(tile_piece[None], (bands, piece, window))
+    everything = exchange(lax.dynamic_update_slice(sums, copies, (0, 4 * deep, 0)), "scan")
     gathered = jnp.sum(everything.astype(F32), axis=0)
     full_piece = gathered[4 * deep:] / math.sqrt(patterns * bands * tiles)
     probe_grad = exchange(

time: 114 us -> 114 us (level)
  transfers between devices with their start and end apart: 5 -> 5, of which waited for: 4 -> 4; matrix products, arithmetic and copies ran while one was open for 2% -> 1% of each run, Pallas kernels for 0% -> 0%
where the time goes in v6:
time: 114 us
  waiting for transfers between devices  46.7 us (41%)
  starting transfers between devices  32 us (28%)
  blocking collectives  16.9 us (15%)
  Pallas kernels  13.3 us (12%)
  other arithmetic  2.45 us (2%)
  local copies, waits for them, and re-layouts  1.69 us (1%)
    all_to_all x3, waiting for transfers between devices, exchange(): return lax.all_to_all(value, axis, split_axis=0, concat_axis=0, tiled=True)  46.5 us
    all_to_all x3, starting transfers between devices, exchange(): return lax.all_to_all(value, axis, split_axis=0, concat_axis=0, tiled=True)  26.4 us
    all_to_all x1, blocking collectives, exchange(): return lax.all_to_all(value, axis, split_axis=0, concat_axis=0, tiled=True)  16.9 us
    pallas_call x1, Pallas kernels, compute(): pl.pallas_call(main_kernel, grid=(1,), out_shape=(jax.ShapeDtypeStruct(pr...  11.1 us
    ppermute x1, starting transfers between devices, local(): lax.ppermute(strips[:, 1], 'tile', [(t, t + 1) for t in range(tiles - 1)])  3.55 us
  transfers between devices with their start and end apart: 5, of which 4 were waited for; matrix products, arithmetic and copies ran while one was open for 1% of the time, Pallas kernels for 0%

profile of v6, /device:TPU:1, one launch (start us, length us, event | category | flops | bytes accessed | tf_op | source)
XLA Modules:
  0.0 113.8 jit_solution(8328101107497896352)
XLA Ops:
  0.6 0.0 copy-start.1
  0.6 0.0 copy-start
  0.7 0.0 copy-start.2
  0.7 2.2 %shard_map.76 = s16[16,144,128]{2,1,0:T(8,128)(2,1)} custom-call(s32[2,8]{1,0:T(2,128)} %bitcast.16, f32[8,128,128]{2,1,0:T(8,128)} %measured.1), custom_call_target="tpu_custom_call" | custom-call | tf_op jit(solution)/shard_map/pallas_call | solution.py:213
  2.9 10.3 %all-to-all-start = ((s16[16,144,128]{2,1,0:T(8,128)(2,1)}), s16[16,144,128]{2,1,0:T(8,128)(2,1)S(1)}, u32[]{:S(2)}, u32[]{:S(2)}) async-start(s16[16,144,128]{2,1,0:T(8,128)(2,1)} %shard_map.76), calls=%async_computation | async-start | bytes 1179648 | tf_op jit(solution)/shard_map/all_to_all | solution.py:269
  13.2 0.0 copy-done
  13.2 2.1 %collective-permute-start = (bf16[2,512,128]{2,1,0:T(8,128)(2,1)S(1)}, bf16[2,512,128]{2,1,0:T(8,128)(2,1)S(1)}, u32[]{:S(2)}, u32[]{:S(2)}) collective-permute-start(bf16[2,512,128]{2,1,0:T(8,128)(2,1)S(1)} %slice.63), channel_id=1, source_target_pairs={{1,0},{2,1},{3,2},{4,3},{5,4},{6,5},{7,6},{8,7},{9,8},{10,9},{11,1... | collective-permute-start | bytes 786440 | tf_op jit(solution)/shard_map/ppermute | solution.py:281
  15.4 16.5 %all-to-all-done.received = s16[16,144,128]{2,1,0:T(8,128)(2,1)S(1)} async-done(((s16[16,144,128]{2,1,0:T(8,128)(2,1)}), s16[16,144,128]{2,1,0:T(8,128)(2,1)S(1)}, u32[]{:S(2)}, u32[]{:S(2)}) %all-to-all-start) | async-done | bytes 589856 | tf_op jit(solution)/shard_map/all_to_all | solution.py:269
  31.8 0.0 collective-permute-done.margin
  31.8 0.0 copy-done.1
  31.8 0.0 copy-done.2
  31.8 11.1 %shard_map.77 = (bf16[16,64,128]{2,1,0:T(8,128)(2,1)S(1)}, bf16[32,112,128]{2,1,0:T(8,128)(2,1)}) custom-call(s32[16,3]{1,0:T(8,128)S(1)} %bitcast.13, s16[16,144,128]{2,1,0:T(8,128)(2,1)S(1)} %all-to-all-done.received, f32[2,512,384]{2,1,0:T(8,128)S(1)} %copy-done, bf16[2,512,128]{2,1,0:T(8,128)(2,1)S(1)} %collective-permute-done.margin, ...), custom_call_target="tpu_custom_call" | custom-call | tf_op jit(solution)/shard_map/pallas_call | solution.py:240
  42.9 16.9 %all_to_all.20 = bf16[16,64,128]{2,1,0:T(8,128)(2,1)S(1)} all-to-all(bf16[16,64,128]{2,1,0:T(8,128)(2,1)S(1)} %get-tuple-element.6), channel_id=1, replica_groups=mesh['scan'=32,'tile'=16] {'tile'}, dimensions={0} | all-to-all | bytes 524288 | tf_op jit(solution)/shard_map/all_to_all | solution.py:269
  59.8 0.0 copy-start.3
  59.9 0.8 broadcast_dynamic-update-slice_fusion
  60.7 11.2 %all-to-all-start.2 = ((bf16[32,112,128]{2,1,0:T(8,128)(2,1)}), bf16[32,112,128]{2,1,0:T(8,128)(2,1)S(1)}, u32[]{:S(2)}, u32[]{:S(2)}) async-start(bf16[32,112,128]{2,1,0:T(8,128)(2,1)} %broadcast_dynamic-update-slice_fusion), calls=%async_computation.2 | async-start | bytes 1835008 | tf_op jit(solution)/shard_map/all_to_all | solution.py:269
  72.0 0.0 copy-done.3
  72.0 0.1 iota_compare_fusion
  72.1 0.1 fusion.1
  72.2 0.1 copy.23
  72.3 24.3 %all-to-all-done.2 = bf16[32,112,128]{2,1,0:T(8,128)(2,1)S(1)} async-done(((bf16[32,112,128]{2,1,0:T(8,128)(2,1)}), bf16[32,112,128]{2,1,0:T(8,128)(2,1)S(1)}, u32[]{:S(2)}, u32[]{:S(2)}) %all-to-all-start.2) | async-done | bytes 917536 | tf_op jit(solution)/shard_map/all_to_all | solution.py:269
  96.6 0.1 convert_reduce_fusion
  96.8 0.7 broadcast_in_dim.41
  97.5 4.9 %all-to-all-start.3 = ((bf16[16,48,128]{2,1,0:T(8,128)(2,1)}), bf16[16,48,128]{2,1,0:T(8,128)(2,1)S(1)}, u32[]{:S(2)}, u32[]{:S(2)}) async-start(bf16[16,48,128]{2,1,0:T(8,128)(2,1)} %broadcast_in_dim.41), calls=%async_computation.3 | async-start | bytes 393216 | tf_op jit(solution)/shard_map/all_to_all | solution.py:269
  102.4 3.5 %collective-permute-start.1 = (f32[2,16,128]{2,1,0:T(8,128)S(1)}, f32[2,16,128]{2,1,0:T(8,128)S(1)}, u32[]{:S(2)}, u32[]{:S(2)}) collective-permute-start(f32[2,16,128]{2,1,0:T(8,128)S(1)} %get-tuple-element.7), channel_id=1, source_target_pairs={{0,1},{1,2},{2,3},{3,4},{4,5},{5,6},{6,7},{7,8},{8,9},{9,10},{10,1... | collective-permute-start | bytes 49160 | tf_op jit(solution)/shard_map/ppermute | solution.py:297
  105.9 0.7 select_reduce_fusion
  106.6 0.2 collective-permute-done.1
  106.8 0.6 pad_maximum_fusion
  107.4 5.7 %all-to-all-done.3 = bf16[16,48,128]{2,1,0:T(8,128)(2,1)S(1)} async-done(((bf16[16,48,128]{2,1,0:T(8,128)(2,1)}), bf16[16,48,128]{2,1,0:T(8,128)(2,1)S(1)}, u32[]{:S(2)}, u32[]{:S(2)}) %all-to-all-start.3) | async-done | bytes 196640 | tf_op jit(solution)/shard_map/all_to_all | solution.py:269
  113.1 0.8 convert.6
  (11 shorter events, 0.2 us)
Async XLA Ops:
  0.6 31.2 %copy-start.1 = (bf16[4,256,256]{2,1,0:T(8,128)(2,1)S(1)}, bf16[4,256,256]{2,1,0:T(8,128)(2,1)}, u32[]{:S(2)}) copy-start(bf16[4,256,256]{2,1,0:T(8,128)(2,1)} %constant.25.clone.tables) | copy-start | bytes 1572868
  0.6 12.5 %copy-start = (f32[2,512,384]{2,1,0:T(8,128)S(1)}, f32[2,512,384]{2,1,0:T(8,128)}, u32[]{:S(2)}) copy-start(f32[2,512,384]{2,1,0:T(8,128)} %own.1) | copy-start | bytes 4718596
  0.7 31.2 %copy-start.2 = (bf16[3,2,128,128]{3,2,1,0:T(8,128)(2,1)S(1)}, bf16[3,2,128,128]{3,2,1,0:T(8,128)(2,1)}, u32[]{:S(2)}) copy-start(bf16[3,2,128,128]{3,2,1,0:T(8,128)(2,1)} %probe.1) | copy-start | bytes 589828
  2.9 28.9 %all-to-all-start = ((s16[16,144,128]{2,1,0:T(8,128)(2,1)}), s16[16,144,128]{2,1,0:T(8,128)(2,1)S(1)}, u32[]{:S(2)}, u32[]{:S(2)}) async-start(s16[16,144,128]{2,1,0:T(8,128)(2,1)} %shard_map.76), calls=%async_computation | async-start | bytes 1179648 | tf_op jit(solution)/shard_map/all_to_all | solution.py:269
  13.2 18.6 %collective-permute-start = (bf16[2,512,128]{2,1,0:T(8,128)(2,1)S(1)}, bf16[2,512,128]{2,1,0:T(8,128)(2,1)S(1)}, u32[]{:S(2)}, u32[]{:S(2)}) collective-permute-start(bf16[2,512,128]{2,1,0:T(8,128)(2,1)S(1)} %slice.63), channel_id=1, source_target_pairs={{1,0},{2,1},{3,2},{4,3},{5,4},{6,5},{7,6},{8,7},{9,8},{10,9},{11,1... | collective-permute-start | bytes 786440 | tf_op jit(solution)/shard_map/ppermute | solution.py:281
  59.8 12.2 %copy-start.3 = (s32[8,2]{0,1:T(2,128)S(1)}, s32[8,2]{0,1:T(2,128)}, u32[]{:S(2)}) copy-start(s32[8,2]{0,1:T(2,128)} %param.8) | copy-start | bytes 196
  60.7 35.9 %all-to-all-start.2 = ((bf16[32,112,128]{2,1,0:T(8,128)(2,1)}), bf16[32,112,128]{2,1,0:T(8,128)(2,1)S(1)}, u32[]{:S(2)}, u32[]{:S(2)}) async-start(bf16[32,112,128]{2,1,0:T(8,128)(2,1)} %broadcast_dynamic-update-slice_fusion), calls=%async_computation.2 | async-start | bytes 1835008 | tf_op jit(solution)/shard_map/all_to_all | solution.py:269
  97.5 15.6 %all-to-all-start.3 = ((bf16[16,48,128]{2,1,0:T(8,128)(2,1)}), bf16[16,48,128]{2,1,0:T(8,128)(2,1)S(1)}, u32[]{:S(2)}, u32[]{:S(2)}) async-start(bf16[16,48,128]{2,1,0:T(8,128)(2,1)} %broadcast_in_dim.41), calls=%async_computation.3 | async-start | bytes 393216 | tf_op jit(solution)/shard_map/all_to_all | solution.py:269
  102.4 4.4 %collective-permute-start.1 = (f32[2,16,128]{2,1,0:T(8,128)S(1)}, f32[2,16,128]{2,1,0:T(8,128)S(1)}, u32[]{:S(2)}, u32[]{:S(2)}) collective-permute-start(f32[2,16,128]{2,1,0:T(8,128)S(1)} %get-tuple-element.7), channel_id=1, source_target_pairs={{0,1},{1,2},{2,3},{3,4},{4,5},{5,6},{6,7},{7,8},{8,9},{9,10},{10,1... | collective-permute-start | bytes 49160 | tf_op jit(solution)/shard_map/ppermute | solution.py:297

commit v7 on v6

--- a/solution.py
+++ b/solution.py
@@ -236,7 +236,7 @@
         return pl.BlockSpec(shape, lambda i: (0,) * len(shape))
 
     probe_shape = (slots, 2 * modes * window // slots + 16, window)
-    sums_shape = (bands, 4 * (height // bands) + 2 * modes * window // slots, window)
+    sums_shape = (bands, 4 * (height // bands), window)
     return pl.pallas_call(
         main_kernel,
         grid=(1,),
@@ -286,8 +286,10 @@
     probe_sums, sums = compute(notes, received, object_field, margin, probe, bands)
     mixed = exchange(probe_sums, "tile").astype(F32)
     tile_piece = jnp.sum(mixed[:, :piece], axis=0).astype(BF16)
-    copies = jnp.broadcast_to(tile_piece[None], (bands, piece, window))
-    everything = exchange(lax.dynamic_update_slice(sums, copies, (0, 4 * deep, 0)), "scan")
+    everything = exchange(
+        jnp.concatenate([sums, jnp.broadcast_to(tile_piece[None], (bands, piece, window))], axis=1),
+        "scan",
+    )
     gathered = jnp.sum(everything.astype(F32), axis=0)
     full_piece = gathered[4 * deep:] / math.sqrt(patterns * bands * tiles)
     probe_grad = exchange(

time: 114 us -> 113 us (level)
  no operation moved by 1% of the time
where the time goes in v7:
time: 113 us
  waiting for transfers between devices  46.7 us (41%)
  starting transfers between devices  32 us (28%)
  blocking collectives  16.8 us (15%)
  Pallas kernels  12.4 us (11%)
  other arithmetic  3.43 us (3%)
    all_to_all x3, waiting for transfers between devices, exchange(): return lax.all_to_all(value, axis, split_axis=0, concat_axis=0, tiled=True)  46.5 us
    all_to_all x3, starting transfers between devices, exchange(): return lax.all_to_all(value, axis, split_axis=0, concat_axis=0, tiled=True)  26.4 us
    all_to_all x1, blocking collectives, exchange(): return lax.all_to_all(value, axis, split_axis=0, concat_axis=0, tiled=True)  16.8 us
    pallas_call x1, Pallas kernels, compute(): pl.pallas_call(main_kernel, grid=(1,), out_shape=(jax.ShapeDtypeStruct(pr...  10.1 us
    ppermute x1, starting transfers between devices, local(): lax.ppermute(strips[:, 1], 'tile', [(t, t + 1) for t in range(tiles - 1)])  3.55 us
  transfers between devices with their start and end apart: 5, of which 4 were waited for; matrix products, arithmetic and copies ran while one was open for 1% of the time, Pallas kernels for 0%

profile of v7, /device:TPU:1, one launch (start us, length us, event | category | flops | bytes accessed | tf_op | source)
XLA Modules:
  0.0 113.0 jit_solution(3421047118044694294)
XLA Ops:
  0.6 0.0 copy-start.1
  0.6 0.0 copy-start
  0.7 0.0 copy-start.2
  0.7 2.2 %shard_map.76 = s16[16,144,128]{2,1,0:T(8,128)(2,1)} custom-call(s32[2,8]{1,0:T(2,128)} %bitcast.16, f32[8,128,128]{2,1,0:T(8,128)} %measured.1), custom_call_target="tpu_custom_call" | custom-call | tf_op jit(solution)/shard_map/pallas_call | solution.py:213
  2.9 10.3 %all-to-all-start = ((s16[16,144,128]{2,1,0:T(8,128)(2,1)}), s16[16,144,128]{2,1,0:T(8,128)(2,1)S(1)}, u32[]{:S(2)}, u32[]{:S(2)}) async-start(s16[16,144,128]{2,1,0:T(8,128)(2,1)} %shard_map.76), calls=%async_computation | async-start | bytes 1179648 | tf_op jit(solution)/shard_map/all_to_all | solution.py:269
  13.2 0.0 copy-done
  13.2 2.1 %collective-permute-start = (bf16[2,512,128]{2,1,0:T(8,128)(2,1)S(1)}, bf16[2,512,128]{2,1,0:T(8,128)(2,1)S(1)}, u32[]{:S(2)}, u32[]{:S(2)}) collective-permute-start(bf16[2,512,128]{2,1,0:T(8,128)(2,1)S(1)} %slice.63), channel_id=1, source_target_pairs={{1,0},{2,1},{3,2},{4,3},{5,4},{6,5},{7,6},{8,7},{9,8},{10,9},{11,1... | collective-permute-start | bytes 786440 | tf_op jit(solution)/shard_map/ppermute | solution.py:281
  15.4 16.5 %all-to-all-done.received = s16[16,144,128]{2,1,0:T(8,128)(2,1)S(1)} async-done(((s16[16,144,128]{2,1,0:T(8,128)(2,1)}), s16[16,144,128]{2,1,0:T(8,128)(2,1)S(1)}, u32[]{:S(2)}, u32[]{:S(2)}) %all-to-all-start) | async-done | bytes 589856 | tf_op jit(solution)/shard_map/all_to_all | solution.py:269
  31.8 0.0 collective-permute-done.margin
  31.8 0.0 copy-done.1
  31.8 0.0 copy-done.2
  31.8 10.1 %shard_map.77 = (bf16[16,64,128]{2,1,0:T(8,128)(2,1)S(1)}, bf16[32,64,128]{2,1,0:T(8,128)(2,1)S(1)}) custom-call(s32[16,3]{1,0:T(8,128)S(1)} %bitcast.13, s16[16,144,128]{2,1,0:T(8,128)(2,1)S(1)} %all-to-all-done.received, f32[2,512,384]{2,1,0:T(8,128)S(1)} %copy-done, bf16[2,512,128]{2,1,0:T(8,128)(2,1)S(1)} %collective-permute-done.margin, ...), custom_call_target="tpu_custom_call" | custom-call | tf_op jit(solution)/shard_map/pallas_call | solution.py:240
  42.0 16.8 %all_to_all.20 = bf16[16,64,128]{2,1,0:T(8,128)(2,1)S(1)} all-to-all(bf16[16,64,128]{2,1,0:T(8,128)(2,1)S(1)} %get-tuple-element.6), channel_id=1, replica_groups=mesh['scan'=32,'tile'=16] {'tile'}, dimensions={0} | all-to-all | bytes 524288 | tf_op jit(solution)/shard_map/all_to_all | solution.py:269
  58.9 0.1 broadcast_in_dim.19
  58.9 0.0 copy-start.3
  58.9 1.0 pad_maximum_fusion
  59.9 11.2 %all-to-all-start.2 = ((bf16[32,112,128]{2,1,0:T(8,128)(2,1)}), bf16[32,112,128]{2,1,0:T(8,128)(2,1)S(1)}, u32[]{:S(2)}, u32[]{:S(2)}) async-start(bf16[32,112,128]{2,1,0:T(8,128)(2,1)} %pad_maximum_fusion), calls=%async_computation.2 | async-start | bytes 1835008 | tf_op jit(solution)/shard_map/all_to_all | solution.py:269
  71.2 0.0 copy-done.3
  71.2 0.1 iota_compare_fusion
  71.3 0.1 fusion.1
  71.4 0.1 copy.23
  71.5 24.3 %all-to-all-done.2 = bf16[32,112,128]{2,1,0:T(8,128)(2,1)S(1)} async-done(((bf16[32,112,128]{2,1,0:T(8,128)(2,1)}), bf16[32,112,128]{2,1,0:T(8,128)(2,1)S(1)}, u32[]{:S(2)}, u32[]{:S(2)}) %all-to-all-start.2) | async-done | bytes 917536 | tf_op jit(solution)/shard_map/all_to_all | solution.py:269
  95.8 0.1 convert_reduce_fusion
  96.0 0.7 broadcast_in_dim.41
  96.7 4.9 %all-to-all-start.3 = ((bf16[16,48,128]{2,1,0:T(8,128)(2,1)}), bf16[16,48,128]{2,1,0:T(8,128)(2,1)S(1)}, u32[]{:S(2)}, u32[]{:S(2)}) async-start(bf16[16,48,128]{2,1,0:T(8,128)(2,1)} %broadcast_in_dim.41), calls=%async_computation.3 | async-start | bytes 393216 | tf_op jit(solution)/shard_map/all_to_all | solution.py:269
  101.5 3.5 %collective-permute-start.1 = (f32[2,16,128]{2,1,0:T(8,128)S(1)}, f32[2,16,128]{2,1,0:T(8,128)S(1)}, u32[]{:S(2)}, u32[]{:S(2)}) collective-permute-start(f32[2,16,128]{2,1,0:T(8,128)S(1)} %get-tuple-element.7), channel_id=1, source_target_pairs={{0,1},{1,2},{2,3},{3,4},{4,5},{5,6},{6,7},{7,8},{8,9},{9,10},{10,1... | collective-permute-start | bytes 49160 | tf_op jit(solution)/shard_map/ppermute | solution.py:299
  105.1 0.7 select_reduce_fusion
  105.7 0.2 collective-permute-done.1
  105.9 0.6 pad_maximum_fusion.1
  106.6 5.7 %all-to-all-done.3 = bf16[16,48,128]{2,1,0:T(8,128)(2,1)S(1)} async-done(((bf16[16,48,128]{2,1,0:T(8,128)(2,1)}), bf16[16,48,128]{2,1,0:T(8,128)(2,1)S(1)}, u32[]{:S(2)}, u32[]{:S(2)}) %all-to-all-start.3) | async-done | bytes 196640 | tf_op jit(solution)/shard_map/all_to_all | solution.py:269
  112.2 0.8 convert.6
  (11 shorter events, 0.2 us)
Async XLA Ops:
  0.6 31.2 %copy-start.1 = (bf16[4,256,256]{2,1,0:T(8,128)(2,1)S(1)}, bf16[4,256,256]{2,1,0:T(8,128)(2,1)}, u32[]{:S(2)}) copy-start(bf16[4,256,256]{2,1,0:T(8,128)(2,1)} %constant.22.clone.tables) | copy-start | bytes 1572868
  0.6 12.5 %copy-start = (f32[2,512,384]{2,1,0:T(8,128)S(1)}, f32[2,512,384]{2,1,0:T(8,128)}, u32[]{:S(2)}) copy-start(f32[2,512,384]{2,1,0:T(8,128)} %own.1) | copy-start | bytes 4718596
  0.7 31.2 %copy-start.2 = (bf16[3,2,128,128]{3,2,1,0:T(8,128)(2,1)S(1)}, bf16[3,2,128,128]{3,2,1,0:T(8,128)(2,1)}, u32[]{:S(2)}) copy-start(bf16[3,2,128,128]{3,2,1,0:T(8,128)(2,1)} %probe.1) | copy-start | bytes 589828
  2.9 28.9 %all-to-all-start = ((s16[16,144,128]{2,1,0:T(8,128)(2,1)}), s16[16,144,128]{2,1,0:T(8,128)(2,1)S(1)}, u32[]{:S(2)}, u32[]{:S(2)}) async-start(s16[16,144,128]{2,1,0:T(8,128)(2,1)} %shard_map.76), calls=%async_computation | async-start | bytes 1179648 | tf_op jit(solution)/shard_map/all_to_all | solution.py:269
  13.2 18.6 %collective-permute-start = (bf16[2,512,128]{2,1,0:T(8,128)(2,1)S(1)}, bf16[2,512,128]{2,1,0:T(8,128)(2,1)S(1)}, u32[]{:S(2)}, u32[]{:S(2)}) collective-permute-start(bf16[2,512,128]{2,1,0:T(8,128)(2,1)S(1)} %slice.63), channel_id=1, source_target_pairs={{1,0},{2,1},{3,2},{4,3},{5,4},{6,5},{7,6},{8,7},{9,8},{10,9},{11,1... | collective-permute-start | bytes 786440 | tf_op jit(solution)/shard_map/ppermute | solution.py:281
  58.9 12.3 %copy-start.3 = (s32[8,2]{0,1:T(2,128)S(1)}, s32[8,2]{0,1:T(2,128)}, u32[]{:S(2)}) copy-start(s32[8,2]{0,1:T(2,128)} %param.8) | copy-start | bytes 196
  59.9 35.9 %all-to-all-start.2 = ((bf16[32,112,128]{2,1,0:T(8,128)(2,1)}), bf16[32,112,128]{2,1,0:T(8,128)(2,1)S(1)}, u32[]{:S(2)}, u32[]{:S(2)}) async-start(bf16[32,112,128]{2,1,0:T(8,128)(2,1)} %pad_maximum_fusion), calls=%async_computation.2 | async-start | bytes 1835008 | tf_op jit(solution)/shard_map/all_to_all | solution.py:269
  96.7 15.6 %all-to-all-start.3 = ((bf16[16,48,128]{2,1,0:T(8,128)(2,1)}), bf16[16,48,128]{2,1,0:T(8,128)(2,1)S(1)}, u32[]{:S(2)}, u32[]{:S(2)}) async-start(bf16[16,48,128]{2,1,0:T(8,128)(2,1)} %broadcast_in_dim.41), calls=%async_computation.3 | async-start | bytes 393216 | tf_op jit(solution)/shard_map/all_to_all | solution.py:269
  101.5 4.4 %collective-permute-start.1 = (f32[2,16,128]{2,1,0:T(8,128)S(1)}, f32[2,16,128]{2,1,0:T(8,128)S(1)}, u32[]{:S(2)}, u32[]{:S(2)}) collective-permute-start(f32[2,16,128]{2,1,0:T(8,128)S(1)} %get-tuple-element.7), channel_id=1, source_target_pairs={{0,1},{1,2},{2,3},{3,4},{4,5},{5,6},{6,7},{7,8},{8,9},{9,10},{10,1... | collective-permute-start | bytes 49160 | tf_op jit(solution)/shard_map/ppermute | solution.py:299

commit v8 on v7

--- a/solution.py
+++ b/solution.py
@@ -75,20 +75,17 @@
 
 def main_kernel(
     notes, received, own, margin, probe, tables,
-    probe_sums, sums, shifts, strip, total, probe_total, probe_full,
+    probe_sums, patches, shifts, strip, probe_total, probe_full,
     probe_near, probe_sem,
 ):
     slots = received.shape[0]
     modes = probe.shape[0]
     window = probe.shape[2]
-    bands = sums.shape[0]
-    height = own.shape[1]
     fetch = pltpu.make_async_copy(probe, probe_near, probe_sem)
     fetch.start()
     for part in range(2):
         strip[part, 0] = own[part].astype(BF16).astype(F32)
         strip[part, 1] = margin[part].astype(F32)
-    total[...] = jnp.zeros(total.shape, F32)
     probe_total[...] = jnp.zeros(probe_total.shape, F32)
     fetch.wait()
     probe_full[...] = probe_near[...].astype(F32)
@@ -124,8 +121,6 @@
         return notes[slot, 2].astype(F32) * (1.0 - amplitude * lax.rsqrt(jnp.maximum(power, 0.25)))
 
     def finish(slot, w_re, w_im, back):
-        start = jnp.clip(notes[slot, 1], 1, window - 1)
-        rows = pl.ds(notes[slot, 0], window)
         patch_re = jnp.zeros((window, window), F32)
         patch_im = jnp.zeros((window, window), F32)
         for m in range(modes):
@@ -141,10 +136,8 @@
             )
             change = jnp.where(at < window - 1, change, 0.0)
             shifts[slot, pl.ds(axis, 1), :] = jnp.sum(change, axis=0, keepdims=True)
-        for part, patch in enumerate((patch_re, patch_im)):
-            turned = pltpu.roll(patch.astype(BF16).astype(F32), start, 1)
-            total[part, 0, rows, :] += jnp.where(lane >= start, turned, 0.0)
-            total[part, 1, rows, :] += jnp.where(lane < start, turned, 0.0)
+        patches[slot, 0] = patch_re.astype(BF16)
+        patches[slot, 1] = patch_im.astype(BF16)
 
     def joined(at, axis):
         return jnp.concatenate([tables[2 * at], tables[2 * at + 1]], axis=axis)
@@ -191,12 +184,6 @@
         for at, flow in enumerate(flows):
             if 0 <= tick - LAG * at < 5:
                 next(flow, None)
-    for b in range(bands):
-        deep = height // bands
-        for part in range(2):
-            for side in range(2):
-                at = (2 * part + side) * deep
-                sums[b, at:at + deep, :] = total[part, side, b * deep:(b + 1) * deep, :].astype(BF16)
     piece = 2 * modes * window // slots
     for t in range(slots):
         mode, offset = divmod(t * piece, window)
@@ -225,7 +212,7 @@
     )(positions.T, measured)
 
 
-def compute(notes, received, object_field, margin, probe, bands):
+def compute(notes, received, object_field, margin, probe):
     modes, window = probe.shape[0], probe.shape[2]
     slots = received.shape[0]
     height = object_field.shape[1]
@@ -236,13 +223,12 @@
         return pl.BlockSpec(shape, lambda i: (0,) * len(shape))
 
     probe_shape = (slots, 2 * modes * window // slots + 16, window)
-    sums_shape = (bands, 4 * (height // bands), window)
     return pl.pallas_call(
         main_kernel,
         grid=(1,),
         out_shape=(
             jax.ShapeDtypeStruct(probe_shape, BF16),
-            jax.ShapeDtypeStruct(sums_shape, BF16),
+            jax.ShapeDtypeStruct((slots, 2, window, window), BF16),
         ),
         in_specs=[
             pl.BlockSpec(memory_space=pltpu.SMEM),
@@ -251,18 +237,53 @@
             whole(margin.shape),
             pl.BlockSpec(memory_space=pltpu.HBM),
         ] + [whole(table.shape) for table in tables],
-        out_specs=(whole(probe_shape), whole(sums_shape)),
+        out_specs=(whole(probe_shape), whole((slots, 2, window, window))),
         scratch_shapes=[
             pltpu.VMEM((slots, 8, window), F32),
-            pltpu.VMEM((2, 2, height, window), F32),
             pltpu.VMEM((2, 2, height, window), F32),
             pltpu.VMEM((2 * modes, window, window), F32),
             pltpu.VMEM((modes, 2, window, window), F32),
             pltpu.VMEM((modes, 2, window, window), BF16),
             pltpu.SemaphoreType.DMA,
         ],
-        compiler_params=pltpu.CompilerParams(vmem_limit_bytes=40 * 2**20),
+        compiler_params=pltpu.CompilerParams(vmem_limit_bytes=59 * 2**20),
     )(notes, received, object_field, margin, probe, *tables)
+
+
+def deposit_kernel(notes, patches, sums, total):
+    slots, window = patches.shape[0], patches.shape[3]
+    bands = sums.shape[0]
+    deep = sums.shape[1] // 4
+    lane = lax.broadcasted_iota(jnp.int32, (window, window), 1)
+    total[...] = jnp.zeros(total.shape, F32)
+    for slot in range(slots):
+        start = jnp.clip(notes[slot, 1], 1, window - 1)
+        rows = pl.ds(notes[slot, 0], window)
+        for part in range(2):
+            turned = pltpu.roll(patches[slot, part].astype(F32), start, 1)
+            total[part, 0, rows, :] += jnp.where(lane >= start, turned, 0.0)
+            total[part, 1, rows, :] += jnp.where(lane < start, turned, 0.0)
+    for b in range(bands):
+        for part in range(2):
+            for side in range(2):
+                at = (2 * part + side) * deep
+                sums[b, at:at + deep, :] = total[part, side, b * deep:(b + 1) * deep, :].astype(BF16)
+
+
+def deposit(notes, patches, bands, height):
+    window = patches.shape[3]
+    return pl.pallas_call(
+        deposit_kernel,
+        out_shape=jax.ShapeDtypeStruct((bands, 4 * (height // bands), window), BF16),
+        in_specs=[
+            pl.BlockSpec(memory_space=pltpu.SMEM),
+            pl.BlockSpec(memory_space=pltpu.VMEM),
+        ],
+        out_specs=pl.BlockSpec(memory_space=pltpu.VMEM),
+        scratch_shapes=[pltpu.VMEM((2, 2, height, window), F32)],
+        compiler_params=pltpu.CompilerParams(vmem_limit_bytes=16 * 2**20),
+        cost_estimate=pl.CostEstimate(flops=4_000_000, bytes_accessed=8_000_000, transcendentals=0),
+    )(notes, patches)
 
 
 def exchange(value, axis):
@@ -283,7 +304,8 @@
     )
     received = exchange(pack(positions, measured, tiles), "tile")
     notes = received[:, window, :3].astype(jnp.int32)
-    probe_sums, sums = compute(notes, received, object_field, margin, probe, bands)
+    probe_sums, patches = compute(notes, received, object_field, margin, probe)
+    sums = deposit(notes, patches, bands, height)
     mixed = exchange(probe_sums, "tile").astype(F32)
     tile_piece = jnp.sum(mixed[:, :piece], axis=0).astype(BF16)
     everything = exchange(

time: 113 us -> 116 us (1.027)
  blocking collectives: 16.8 us -> 0 us
  waiting for transfers between devices: 46.7 us -> 54.9 us
  starting transfers between devices: 32 us -> 36.6 us
  Pallas kernels: 12.4 us -> 15.5 us
  local copies, waits for them, and re-layouts: 0.91 us -> 3.86 us
    all_to_all x1 -> x0, blocking collectives: 16.8 us -> none  [exchange(): return lax.all_to_all(value, axis, split_axis=0, concat_axis=0, tiled=True)]
    all_to_all x3 -> x4, waiting for transfers between devices: 46.5 us -> 54.7 us  [exchange(): return lax.all_to_all(value, axis, split_axis=0, concat_axis=0, tiled=True)]
    all_to_all x3 -> x4, starting transfers between devices: 26.4 us -> 31 us  [exchange(): return lax.all_to_all(value, axis, split_axis=0, concat_axis=0, tiled=True)]
    pallas_call x1, Pallas kernels: 10.1 us -> 12.1 us  [compute(): pl.pallas_call(main_kernel, grid=(1,), out_shape=(jax.ShapeDtypeStruct(pr...]
    unnamed x8 -> x10, local copies, waits for them, and re-layouts: 0.02 us -> 1.93 us
    pallas_call x0 -> x1, Pallas kernels: none -> 1.24 us  [deposit(): pl.pallas_call(deposit_kernel, out_shape=jax.ShapeDtypeStruct((bands, 4 *...]
  transfers between devices with their start and end apart: 5 -> 6, of which waited for: 4 -> 5; matrix products, arithmetic and copies ran while one was open for 1% -> 3% of each run, Pallas kernels for 0% -> 1%
where the time goes in v8:
time: 116 us
  waiting for transfers between devices  54.9 us (47%)
  starting transfers between devices  36.6 us (32%)
  Pallas kernels  15.5 us (13%)
  other arithmetic  4.1 us (4%)
  local copies, waits for them, and re-layouts  3.86 us (3%)
    all_to_all x4, waiting for transfers between devices, exchange(): return lax.all_to_all(value, axis, split_axis=0, concat_axis=0, tiled=True)  54.7 us
    all_to_all x4, starting transfers between devices, exchange(): return lax.all_to_all(value, axis, split_axis=0, concat_axis=0, tiled=True)  31 us
    pallas_call x1, Pallas kernels, compute(): pl.pallas_call(main_kernel, grid=(1,), out_shape=(jax.ShapeDtypeStruct(pr...  12.1 us
    ppermute x1, starting transfers between devices, local(): lax.ppermute(strips[:, 1], 'tile', [(t, t + 1) for t in range(tiles - 1)])  3.55 us
  transfers between devices with their start and end apart: 6, of which 5 were waited for; matrix products, arithmetic and copies ran while one was open for 3% of the time, Pallas kernels for 1%

profile of v8, /device:TPU:1, one launch (start us, length us, event | category | flops | bytes accessed | tf_op | source)
XLA Modules:
  0.0 115.7 jit_solution(3076340705926758363)
XLA Ops:
  0.6 2.1 %shard_map.76 = s16[16,144,128]{2,1,0:T(8,128)(2,1)} custom-call(s32[2,8]{1,0:T(2,128)} %bitcast.17, f32[8,128,128]{2,1,0:T(8,128)} %measured.1), custom_call_target="tpu_custom_call" | custom-call | tf_op jit(solution)/shard_map/pallas_call | solution.py:200
  2.7 10.3 %all-to-all-start = ((s16[16,144,128]{2,1,0:T(8,128)(2,1)}), s16[16,144,128]{2,1,0:T(8,128)(2,1)S(1)}, u32[]{:S(2)}, u32[]{:S(2)}) async-start(s16[16,144,128]{2,1,0:T(8,128)(2,1)} %shard_map.76), calls=%async_computation | async-start | bytes 1179648 | tf_op jit(solution)/shard_map/all_to_all | solution.py:290
  13.0 1.1 slice.63
  14.1 2.1 %collective-permute-start = (bf16[2,512,128]{2,1,0:T(8,128)(2,1)S(1)}, bf16[2,512,128]{2,1,0:T(8,128)(2,1)S(1)}, u32[]{:S(2)}, u32[]{:S(2)}) collective-permute-start(bf16[2,512,128]{2,1,0:T(8,128)(2,1)S(1)} %slice.63), channel_id=1, source_target_pairs={{1,0},{2,1},{3,2},{4,3},{5,4},{6,5},{7,6},{8,7},{9,8},{10,9},{11,1... | collective-permute-start | bytes 786440 | tf_op jit(solution)/shard_map/ppermute | solution.py:302
  16.2 15.4 %all-to-all-done.received = s16[16,144,128]{2,1,0:T(8,128)(2,1)S(1)} async-done(((s16[16,144,128]{2,1,0:T(8,128)(2,1)}), s16[16,144,128]{2,1,0:T(8,128)(2,1)S(1)}, u32[]{:S(2)}, u32[]{:S(2)}) %all-to-all-start) | async-done | bytes 589856 | tf_op jit(solution)/shard_map/all_to_all | solution.py:290
  31.6 0.7 slice_convert_fusion.1
  32.3 0.0 collective-permute-done.margin
  32.3 0.2 copy-done.2
  32.5 0.5 copy-done.3
  33.0 12.1 %shard_map.77 = (bf16[16,64,128]{2,1,0:T(8,128)(2,1)}, bf16[16,2,128,128]{3,2,1,0:T(8,128)(2,1)}) custom-call(s32[16,3]{1,0:T(8,128)} %bitcast.13, s16[16,144,128]{2,1,0:T(8,128)(2,1)} %copy-done.2, f32[2,512,384]{2,1,0:T(8,128)} %own.1, bf16[2,512,128]{2,1,0:T(8,128)(2,1)} %copy-done.3, bf16[3,2,128,128]{3,2,1,0:T(8,128)(2,1)} %probe.1, ...), custom_call_target="tpu_custom_call" | custom-call | tf_op jit(solution)/shard_map/pallas_call | solution.py:226
  45.1 4.6 %all-to-all-start.1 = ((bf16[16,64,128]{2,1,0:T(8,128)(2,1)}), bf16[16,64,128]{2,1,0:T(8,128)(2,1)S(1)}, u32[]{:S(2)}, u32[]{:S(2)}) async-start(bf16[16,64,128]{2,1,0:T(8,128)(2,1)} %get-tuple-element.6), calls=%async_computation.1 | async-start | bytes 524288 | tf_op jit(solution)/shard_map/all_to_all | solution.py:290
  49.8 0.0 copy-start
  49.8 1.2 %copy-done = bf16[16,2,128,128]{3,2,1,0:T(8,128)(2,1)S(1)} copy-done((bf16[16,2,128,128]{3,2,1,0:T(8,128)(2,1)S(1)}, bf16[16,2,128,128]{3,2,1,0:T(8,128)(2,1)}, u32[]{:S(2)}) %copy-start) | copy-done | bytes 1048600
  51.0 1.2 %shard_map.78 = bf16[32,64,128]{2,1,0:T(8,128)(2,1)S(1)} custom-call(s32[16,3]{1,0:T(8,128)S(1)} %bitcast.14, bf16[16,2,128,128]{3,2,1,0:T(8,128)(2,1)S(1)} %copy-done), custom_call_target="tpu_custom_call" | custom-call | flops 4000000 | bytes 8000000 | tf_op jit(solution)/shard_map/pallas_call | solution.py:275
  52.2 9.2 %all-to-all-done.1 = bf16[16,64,128]{2,1,0:T(8,128)(2,1)S(1)} async-done(((bf16[16,64,128]{2,1,0:T(8,128)(2,1)}), bf16[16,64,128]{2,1,0:T(8,128)(2,1)S(1)}, u32[]{:S(2)}, u32[]{:S(2)}) %all-to-all-start.1) | async-done | bytes 262176 | tf_op jit(solution)/shard_map/all_to_all | solution.py:290
  61.6 0.1 broadcast_in_dim.19
  61.6 0.0 copy-start.4
  61.6 1.0 pad_maximum_fusion
  62.6 11.2 %all-to-all-start.2 = ((bf16[32,112,128]{2,1,0:T(8,128)(2,1)}), bf16[32,112,128]{2,1,0:T(8,128)(2,1)S(1)}, u32[]{:S(2)}, u32[]{:S(2)}) async-start(bf16[32,112,128]{2,1,0:T(8,128)(2,1)} %pad_maximum_fusion), calls=%async_computation.2 | async-start | bytes 1835008 | tf_op jit(solution)/shard_map/all_to_all | solution.py:290
  73.9 0.1 iota_compare_fusion
  74.0 0.1 fusion.1
  74.1 0.1 copy.28
  74.1 24.3 %all-to-all-done.2 = bf16[32,112,128]{2,1,0:T(8,128)(2,1)S(1)} async-done(((bf16[32,112,128]{2,1,0:T(8,128)(2,1)}), bf16[32,112,128]{2,1,0:T(8,128)(2,1)S(1)}, u32[]{:S(2)}, u32[]{:S(2)}) %all-to-all-start.2) | async-done | bytes 917536 | tf_op jit(solution)/shard_map/all_to_all | solution.py:290
  98.5 0.1 convert_reduce_fusion
  98.6 0.7 broadcast_in_dim.41
  99.4 4.9 %all-to-all-start.3 = ((bf16[16,48,128]{2,1,0:T(8,128)(2,1)}), bf16[16,48,128]{2,1,0:T(8,128)(2,1)S(1)}, u32[]{:S(2)}, u32[]{:S(2)}) async-start(bf16[16,48,128]{2,1,0:T(8,128)(2,1)} %broadcast_in_dim.41), calls=%async_computation.3 | async-start | bytes 393216 | tf_op jit(solution)/shard_map/all_to_all | solution.py:290
  104.2 3.5 %collective-permute-start.1 = (f32[2,16,128]{2,1,0:T(8,128)S(1)}, f32[2,16,128]{2,1,0:T(8,128)S(1)}, u32[]{:S(2)}, u32[]{:S(2)}) collective-permute-start(f32[2,16,128]{2,1,0:T(8,128)S(1)} %get-tuple-element.7), channel_id=1, source_target_pairs={{0,1},{1,2},{2,3},{3,4},{4,5},{5,6},{6,7},{7,8},{8,9},{9,10},{10,1... | collective-permute-start | bytes 49160 | tf_op jit(solution)/shard_map/ppermute | solution.py:321
  107.8 0.7 select_reduce_fusion
  108.4 0.2 collective-permute-done.1
  108.6 0.6 pad_maximum_fusion.1
  109.2 5.7 %all-to-all-done.3 = bf16[16,48,128]{2,1,0:T(8,128)(2,1)S(1)} async-done(((bf16[16,48,128]{2,1,0:T(8,128)(2,1)}), bf16[16,48,128]{2,1,0:T(8,128)(2,1)S(1)}, u32[]{:S(2)}, u32[]{:S(2)}) %all-to-all-start.3) | async-done | bytes 196640 | tf_op jit(solution)/shard_map/all_to_all | solution.py:290
  114.9 0.8 convert.6
  (14 shorter events, 0.1 us)
Async XLA Ops:
  2.7 28.9 %all-to-all-start = ((s16[16,144,128]{2,1,0:T(8,128)(2,1)}), s16[16,144,128]{2,1,0:T(8,128)(2,1)S(1)}, u32[]{:S(2)}, u32[]{:S(2)}) async-start(s16[16,144,128]{2,1,0:T(8,128)(2,1)} %shard_map.76), calls=%async_computation | async-start | bytes 1179648 | tf_op jit(solution)/shard_map/all_to_all | solution.py:290
  14.1 18.2 %collective-permute-start = (bf16[2,512,128]{2,1,0:T(8,128)(2,1)S(1)}, bf16[2,512,128]{2,1,0:T(8,128)(2,1)S(1)}, u32[]{:S(2)}, u32[]{:S(2)}) collective-permute-start(bf16[2,512,128]{2,1,0:T(8,128)(2,1)S(1)} %slice.63), channel_id=1, source_target_pairs={{1,0},{2,1},{3,2},{4,3},{5,4},{6,5},{7,6},{8,7},{9,8},{10,9},{11,1... | collective-permute-start | bytes 786440 | tf_op jit(solution)/shard_map/ppermute | solution.py:302
  31.6 0.8 copy-start.2
  32.3 0.7 copy-start.3
  33.0 16.8 %copy-start.1 = (s32[16,1,3]{2,1,0:T(1,128)S(1)}, s32[16,1,3]{2,1,0:T(1,128)}, u32[]{:S(2)}) copy-start(s32[16,1,3]{2,1,0:T(1,128)} %slice_convert_fusion.1) | copy-start | bytes 580
  45.1 16.3 %all-to-all-start.1 = ((bf16[16,64,128]{2,1,0:T(8,128)(2,1)}), bf16[16,64,128]{2,1,0:T(8,128)(2,1)S(1)}, u32[]{:S(2)}, u32[]{:S(2)}) async-start(bf16[16,64,128]{2,1,0:T(8,128)(2,1)} %get-tuple-element.6), calls=%async_computation.1 | async-start | bytes 524288 | tf_op jit(solution)/shard_map/all_to_all | solution.py:290
  49.8 1.2 %copy-start = (bf16[16,2,128,128]{3,2,1,0:T(8,128)(2,1)S(1)}, bf16[16,2,128,128]{3,2,1,0:T(8,128)(2,1)}, u32[]{:S(2)}) copy-start(bf16[16,2,128,128]{3,2,1,0:T(8,128)(2,1)} %get-tuple-element.5.patches) | copy-start | bytes 3145732
  61.6 12.3 %copy-start.4 = (s32[8,2]{0,1:T(2,128)S(1)}, s32[8,2]{0,1:T(2,128)}, u32[]{:S(2)}) copy-start(s32[8,2]{0,1:T(2,128)} %param.8) | copy-start | bytes 196
  62.6 35.9 %all-to-all-start.2 = ((bf16[32,112,128]{2,1,0:T(8,128)(2,1)}), bf16[32,112,128]{2,1,0:T(8,128)(2,1)S(1)}, u32[]{:S(2)}, u32[]{:S(2)}) async-start(bf16[32,112,128]{2,1,0:T(8,128)(2,1)} %pad_maximum_fusion), calls=%async_computation.2 | async-start | bytes 1835008 | tf_op jit(solution)/shard_map/all_to_all | solution.py:290
  99.4 15.6 %all-to-all-start.3 = ((bf16[16,48,128]{2,1,0:T(8,128)(2,1)}), bf16[16,48,128]{2,1,0:T(8,128)(2,1)S(1)}, u32[]{:S(2)}, u32[]{:S(2)}) async-start(bf16[16,48,128]{2,1,0:T(8,128)(2,1)} %broadcast_in_dim.41), calls=%async_computation.3 | async-start | bytes 393216 | tf_op jit(solution)/shard_map/all_to_all | solution.py:290
  104.2 4.4 %collective-permute-start.1 = (f32[2,16,128]{2,1,0:T(8,128)S(1)}, f32[2,16,128]{2,1,0:T(8,128)S(1)}, u32[]{:S(2)}, u32[]{:S(2)}) collective-permute-start(f32[2,16,128]{2,1,0:T(8,128)S(1)} %get-tuple-element.7), channel_id=1, source_target_pairs={{0,1},{1,2},{2,3},{3,4},{4,5},{5,6},{6,7},{7,8},{8,9},{9,10},{10,1... | collective-permute-start | bytes 49160 | tf_op jit(solution)/shard_map/ppermute | solution.py:321
